TPU v7x, 512 devices: a whole 4x4x16 slice. The times are simulated.
512 devices in a mesh: panel: 64 (over x, z), obs: 8 (over y, core).
Axes of the slice: x: 4, y: 4, z: 16, core: 2. Of those that a mesh axis runs over, the one named last changes fastest.
Arguments:
- donor: bfloat16 [512, 125, 4, 1024], P('panel', None, None, 'obs'), may hold values from -6 to 6
- donor_elem: int32 [8192], P('obs'), may hold values from 0 to 1023, as said below
- local_coords: float32 [3, 8192], P(None, 'obs'), may hold values from -1 to 1
- owner: int32 [8192], replicated, may hold values from 0 to 63, as said below
- weights: bfloat16 [1024, 4, 4, 8192], P('obs', None, None, 'panel'), may hold values from -0.015625 to 0.015625
- offsets: int32 [8, 64], P('obs', 'panel'), may hold values from 0 to 256
Outputs:
- pressure: float32 [512, 1024], P('panel', 'obs')
Inputs may be any that keep to these rules, and one draw needn't show every extreme that they name: `donor_elem`: point i lies in a donor element of the i // 1024-th block of 128 elements. Every owner owns exactly 128 points. Within each of the 8 aligned blocks of 1024 points an owner appears either 44 times or 128 / 8 - 128 / 32 times, and exactly one block holds 44 of its points.
All inputs are finite; a program needn't handle non-finite values.
Results may differ from a plain program's by a relative error of at most 0.0029.
Values may be sent and summed in bfloat16 or wider, within the bound.
A program may use at most 64 MiB of HBM per device.

v0:
```python
import jax
import jax.numpy as jnp
from jax import lax
from jax.sharding import PartitionSpec as P

BAND = 4
OBLK = 128
PTILE = 128


NODE_SPOTS = (-1.0, -0.5, 0.0, 0.5, 1.0)


def lagrange_table(coords):
    factors = []
    for direction in range(3):
        coord_row = coords[direction]
        columns = []
        for node_one in range(5):
            weighting = jnp.ones_like(coord_row)
            for node_two in range(5):
                if node_two != node_one:
                    weighting = weighting * (
                        (coord_row - NODE_SPOTS[node_two])
                        / (NODE_SPOTS[node_one] - NODE_SPOTS[node_two])
                    )
            columns.append(weighting)
        factors.append(jnp.stack(columns))
    node_table = (
        factors[0][:, None, None, :] * factors[1][None, :, None, :] * factors[2][None, None, :, :]
    )
    return node_table.reshape(125, coords.shape[1])


def body(donor, donor_elem, local_coords, owner, weights, offsets):
    share_index = lax.axis_index("obs")
    elem_local = donor_elem - share_index * donor.shape[3]
    node_table = lagrange_table(local_coords)

    def one_time(moment):
        values = jnp.take(moment, elem_local, axis=2)
        return jnp.sum(node_table[:, None, :] * values, axis=0).astype(jnp.bfloat16)

    local_sources = lax.map(one_time, donor)
    order = jnp.argsort(owner, stable=True)
    everything = lax.all_gather(local_sources, "obs", axis=2, tiled=True)
    outgoing = jnp.take(everything, order, axis=2)
    sources = lax.all_to_all(outgoing, "panel", split_axis=2, concat_axis=0, tiled=True)
    total_time = sources.shape[0]
    front = total_time // 2 + BAND - 1
    padded = jnp.pad(sources, ((front, 0), (0, 0), (0, 0)))
    delay_steps = offsets[0, 0]
    base = 0 + front - delay_steps
    stacked = jnp.stack(
        [lax.dynamic_slice_in_dim(padded, base - delay, total_time, 0) for delay in range(BAND)],
        axis=1,
    )
    stacked = stacked.reshape(total_time, BAND * padded.shape[1] * PTILE)
    weight_tile = weights
    weight_tile = weight_tile.reshape(OBLK, stacked.shape[1])
    running = lax.dot_general(
        stacked, weight_tile, (((1,), (1,)), ((), ())), preferred_element_type=jnp.float32
    )
    pressure = lax.psum_scatter(running, "panel", scatter_dimension=0, tiled=True)
    return pressure


def solution(mesh):
    return jax.shard_map(
        body,
        mesh=mesh,
        in_specs=(
            P("panel", None, None, "obs"),
            P("obs"),
            P(None, "obs"),
            P(),
            P("obs", None, None, "panel"),
            P("obs", "panel"),
        ),
        out_specs=P("panel", "obs"),
        check_vma=False,
    )
```

profile of v0, /device:TPU:1, one launch (start us, length us, event | category | flops | bytes accessed | tf_op | source)
XLA Modules:
  0.0 627.2 jit_solution(15393408633668595031)
XLA Ops:
  6.5 7.6 %sort.17 = (s32[8192]{0:T(1024)}, s32[8192]{0:T(1024)S(1)}) sort(s32[8192]{0:T(1024)} %param.11, s32[8192]{0:T(1024)S(1)} %iota.4), dimensions={0}, to_apply=%region_0.1 | sort | flops 106496 | bytes 131072 | tf_op jit(solution)/shard_map/jit(argsort)/sort | solution.py:45
  14.2 1.0 multiply_multiply_fusion.10
  15.1 0.7 broadcast_subtract_fusion
  16.0 160.1 %while.11 = (s32[]{:T(128)}, bf16[8,4,1024]{2,0,1:T(8,128)(2,1)S(1)}, s32[1024]{0:T(1024)S(1)}, bf16[8,125,4,128]{3,2,1,0:T(4,128)(2,1)}, f32[5,1024]{1,0:T(8,12...) while((s32[]{:T(128)}, bf16[8,4,1024]{2,0,1:T(8,128)(2,1)S(1)}, s32[1024]{0:T(1024)S(1)}, ...), condition=%wide.region_3.4_spmd.clone, body=%wide.region_1.0_spmd.clone.sunk | while | flops 2182146 | bytes 6846565 | solution.py:44
  16.0 1.0 constant_dynamic-slice_fusion.3
  17.4 0.2 copy.38
  17.6 3.6 gather_fusion
  21.1 14.5 %fusion.23 = bf16[4,1024]{0,1:T(8,128)(2,1)S(1)} fusion(bf16[1024,125,4]{1,2,0:T(4,128)(2,1)S(1)} %gather_fusion, f32[125,1024]{0,1:T(8,128)S(1)} %copy.38, pred[1024]{0:T(1024)(128)(4,1)S(1)} %compare_and_fusion.3), kind=kLoop, calls=%fused_computation.4.clone.1 | loop fusion | flops 2043904 | bytes 1545216 | tf_op jit(solution)/shard_map/while/body/eval_jaxpr/reduce_sum | solution.py:42
  36.0 1.0 constant_dynamic-slice_fusion.3
  37.4 0.2 copy.38
  37.6 3.6 gather_fusion
  41.2 14.5 %fusion.23 = bf16[4,1024]{0,1:T(8,128)(2,1)S(1)} fusion(bf16[1024,125,4]{1,2,0:T(4,128)(2,1)S(1)} %gather_fusion, f32[125,1024]{0,1:T(8,128)S(1)} %copy.38, pred[1024]{0:T(1024)(128)(4,1)S(1)} %compare_and_fusion.3), kind=kLoop, calls=%fused_computation.4.clone.1 | loop fusion | flops 2043904 | bytes 1545216 | tf_op jit(solution)/shard_map/while/body/eval_jaxpr/reduce_sum | solution.py:42
  56.0 1.0 constant_dynamic-slice_fusion.3
  57.4 0.2 copy.38
  57.6 3.6 gather_fusion
  61.2 14.5 %fusion.23 = bf16[4,1024]{0,1:T(8,128)(2,1)S(1)} fusion(bf16[1024,125,4]{1,2,0:T(4,128)(2,1)S(1)} %gather_fusion, f32[125,1024]{0,1:T(8,128)S(1)} %copy.38, pred[1024]{0:T(1024)(128)(4,1)S(1)} %compare_and_fusion.3), kind=kLoop, calls=%fused_computation.4.clone.1 | loop fusion | flops 2043904 | bytes 1545216 | tf_op jit(solution)/shard_map/while/body/eval_jaxpr/reduce_sum | solution.py:42
  76.1 1.0 constant_dynamic-slice_fusion.3
  77.4 0.2 copy.38
  77.6 3.6 gather_fusion
  81.2 14.5 %fusion.23 = bf16[4,1024]{0,1:T(8,128)(2,1)S(1)} fusion(bf16[1024,125,4]{1,2,0:T(4,128)(2,1)S(1)} %gather_fusion, f32[125,1024]{0,1:T(8,128)S(1)} %copy.38, pred[1024]{0:T(1024)(128)(4,1)S(1)} %compare_and_fusion.3), kind=kLoop, calls=%fused_computation.4.clone.1 | loop fusion | flops 2043904 | bytes 1545216 | tf_op jit(solution)/shard_map/while/body/eval_jaxpr/reduce_sum | solution.py:42
  96.1 1.0 constant_dynamic-slice_fusion.3
  97.6 3.6 gather_fusion
  101.2 14.5 %fusion.23 = bf16[4,1024]{0,1:T(8,128)(2,1)S(1)} fusion(bf16[1024,125,4]{1,2,0:T(4,128)(2,1)S(1)} %gather_fusion, f32[125,1024]{0,1:T(8,128)S(1)} %copy.38, pred[1024]{0:T(1024)(128)(4,1)S(1)} %compare_and_fusion.3), kind=kLoop, calls=%fused_computation.4.clone.1 | loop fusion | flops 2043904 | bytes 1545216 | tf_op jit(solution)/shard_map/while/body/eval_jaxpr/reduce_sum | solution.py:42
  116.1 1.0 constant_dynamic-slice_fusion.3
  117.6 3.6 gather_fusion
  121.2 14.5 %fusion.23 = bf16[4,1024]{0,1:T(8,128)(2,1)S(1)} fusion(bf16[1024,125,4]{1,2,0:T(4,128)(2,1)S(1)} %gather_fusion, f32[125,1024]{0,1:T(8,128)S(1)} %copy.38, pred[1024]{0:T(1024)(128)(4,1)S(1)} %compare_and_fusion.3), kind=kLoop, calls=%fused_computation.4.clone.1 | loop fusion | flops 2043904 | bytes 1545216 | tf_op jit(solution)/shard_map/while/body/eval_jaxpr/reduce_sum | solution.py:42
  136.1 1.0 constant_dynamic-slice_fusion.3
  137.6 3.6 gather_fusion
  141.2 14.5 %fusion.23 = bf16[4,1024]{0,1:T(8,128)(2,1)S(1)} fusion(bf16[1024,125,4]{1,2,0:T(4,128)(2,1)S(1)} %gather_fusion, f32[125,1024]{0,1:T(8,128)S(1)} %copy.38, pred[1024]{0:T(1024)(128)(4,1)S(1)} %compare_and_fusion.3), kind=kLoop, calls=%fused_computation.4.clone.1 | loop fusion | flops 2043904 | bytes 1545216 | tf_op jit(solution)/shard_map/while/body/eval_jaxpr/reduce_sum | solution.py:42
  156.1 1.0 constant_dynamic-slice_fusion.3
  157.4 0.2 copy.38
  157.7 3.6 gather_fusion
  161.2 14.5 %fusion.23 = bf16[4,1024]{0,1:T(8,128)(2,1)S(1)} fusion(bf16[1024,125,4]{1,2,0:T(4,128)(2,1)S(1)} %gather_fusion, f32[125,1024]{0,1:T(8,128)S(1)} %copy.38, pred[1024]{0:T(1024)(128)(4,1)S(1)} %compare_and_fusion.3), kind=kLoop, calls=%fused_computation.4.clone.1 | loop fusion | flops 2043904 | bytes 1545216 | tf_op jit(solution)/shard_map/while/body/eval_jaxpr/reduce_sum | solution.py:42
  176.1 19.8 %all_gather.3 = bf16[8,4,8192]{2,0,1:T(8,128)(2,1)S(1)} all-gather(bf16[8,4,1024]{2,0,1:T(8,128)(2,1)S(1)} %get-tuple-element.34), channel_id=1, replica_groups=mesh['panel'=64,'obs'=8] {'obs'}, dimensions={2}, use_global_device_ids=true | all-gather | bytes 589824 | tf_op jit(solution)/shard_map/all_gather | solution.py:46
  195.9 8.1 %copy.24 = bf16[8,4,8192]{0,1,2:T(4,128)(2,1)} copy(bf16[8,4,8192]{2,0,1:T(8,128)(2,1)S(1)} %all_gather.3) | data formatting | bytes 1048576 | tf_op jit(solution)/shard_map/all_gather | solution.py:46
  204.0 59.6 %gather_fusion.1 = bf16[8192,8,4]{1,2,0:T(4,128)(2,1)} fusion(bf16[8,4,8192]{0,1,2:T(4,128)(2,1)} %copy.24, s32[8192]{0:T(1024)S(1)} %fusion.19), kind=kCustom, calls=%fused_computation.1 | custom fusion | bytes 1081344 | tf_op jit(solution)/shard_map/jit(_take)/gather | solution.py:47
  263.7 30.9 %fusion.21 = bf16[8192,4,8]{2,1,0:T(4,128)(2,1)} fusion(bf16[8192,8,4]{1,2,0:T(4,128)(2,1)} %gather_fusion.1, pred[8192]{0:T(1024)(128)(4,1)S(1)} %compare_and_fusion.1), kind=kLoop, calls=%fused_computation.65 | loop fusion | flops 262144 | bytes 1056768
  294.6 11.2 %reshape.84 = bf16[64,2,2048]{2,1,0:T(2,128)(2,1)} reshape(bf16[8192,4,8]{2,1,0:T(4,128)(2,1)} %fusion.21) | data formatting | bytes 1048576
  305.8 13.5 %all-to-all-start = ((bf16[64,2,2048]{2,1,0:T(2,128)(2,1)}), bf16[64,2,2048]{2,1,0:T(2,128)(2,1)S(1)}, u32[]{:S(2)}, u32[]{:S(2)}) async-start(bf16[64,2,2048]{2,1,0:T(2,128)(2,1)} %reshape.84), calls=%async_computation | async-start | bytes 1048576 | tf_op jit(solution)/shard_map/all_to_all | solution.py:48
  319.3 0.2 all-reduce.4.cloned.1.call-start
  320.2 29.2 %all-to-all-done = bf16[64,2,2048]{2,1,0:T(2,128)(2,1)S(1)} async-done(((bf16[64,2,2048]{2,1,0:T(2,128)(2,1)}), bf16[64,2,2048]{2,1,0:T(2,128)(2,1)S(1)}, u32[]{:S(2)}, u32[]{:S(2)}) %all-to-all-start) | async-done | bytes 524320 | tf_op jit(solution)/shard_map/all_to_all | solution.py:48
  349.4 10.9 %reshape.85 = bf16[8192,4,8]{2,1,0:T(4,128)(2,1)} reshape(bf16[64,2,2048]{2,1,0:T(2,128)(2,1)S(1)} %all-to-all-done) | data formatting | bytes 1048576
  360.2 9.9 %copy.25 = bf16[64,8,4,128]{3,1,0,2:T(8,128)(2,1)S(1)} copy(bf16[64,8,4,128]{1,2,3,0:T(4,128)(2,1)} %bitcast.53) | data formatting | bytes 1048576 | tf_op jit(solution)/shard_map/all_to_all | solution.py:48
  370.1 0.9 fusion.14
  371.0 1.4 fusion.11
  372.4 1.3 dynamic-slice
  374.4 244.7 %all-reduce.4.cloned.1.call-done = f32[512,128]{1,0:T(8,128)} async-done(((f32[512,128]{1,0:T(8,128)}), f32[512,128]{1,0:T(8,128)}) %all-reduce.4.cloned.1.call-update) | async-done | bytes 262160
  619.1 1.3 constant_dynamic-slice_fusion.1
  (78 shorter events, 6.3 us)
Async XLA Ops:
  6.5 364.5 %copy-start = (bf16[128,4,4,128]{3,2,1,0:T(4,128)(2,1)S(1)}, bf16[128,4,4,128]{3,2,1,0:T(4,128)(2,1)}, u32[]{:S(2)}) copy-start(bf16[128,4,4,128]{3,2,1,0:T(4,128)(2,1)} %param.12) | copy-start | bytes 1572868
  305.8 43.6 %all-to-all-start = ((bf16[64,2,2048]{2,1,0:T(2,128)(2,1)}), bf16[64,2,2048]{2,1,0:T(2,128)(2,1)S(1)}, u32[]{:S(2)}, u32[]{:S(2)}) async-start(bf16[64,2,2048]{2,1,0:T(2,128)(2,1)} %reshape.84), calls=%async_computation | async-start | bytes 1048576 | tf_op jit(solution)/shard_map/all_to_all | solution.py:48
  319.3 299.9 %all-reduce.4.cloned.1.call-start = ((), (), s32[]{:S(2)}) async-start(), calls=%async_computation.1 | async-start | bytes 524288
Sparse Core Ops, SparseCore 0:
  372.6 246.5 all-reduce.3
where the time goes:
time: 637 us; the launch traced here: 627 us
  waiting for transfers between devices  274 us (43%)
  other arithmetic  157 us (25%)
  local copies, waits for them, and re-layouts  146 us (23%)
  blocking collectives  19.8 us (3%)
  between operations  14.8 us (2%)
  starting transfers between devices  13.7 us (2%)
    unnamed x2, waiting for transfers between devices  245 us
    reduce_sum x8, other arithmetic, one_time(): return jnp.sum(node_table[:, None, :] * values, axis=0).astype(jnp.bfloat16)  116 us
    gather x1, local copies, waits for them, and re-layouts, body(): outgoing = jnp.take(everything, order, axis=2)  59.6 us
    unnamed x1, other arithmetic  30.9 us
    all_to_all x1, waiting for transfers between devices, body(): lax.all_to_all(outgoing, 'panel', split_axis=2, concat_axis=0, tiled=True)  29.2 us
    gather x8, local copies, waits for them, and re-layouts, one_time(): values = jnp.take(moment, elem_local, axis=2)  28.6 us
    unnamed x6, local copies, waits for them, and re-layouts  24.6 us
    all_gather x1, blocking collectives, body(): everything = lax.all_gather(local_sources, 'obs', axis=2, tiled=True)  19.8 us
  transfers between devices with their start and end apart: 2, of which 2 were waited for; matrix products, arithmetic and copies ran while one was open for 0% of the time, Pallas kernels for 0%

commit v1 on v0

v1 whole, which is shorter than its diff:
```python
import functools

import jax
import jax.numpy as jnp
from jax import lax
from jax.experimental import pallas as pl
from jax.experimental.pallas import tpu as pltpu
from jax.sharding import PartitionSpec as P

F32 = jnp.float32
BF16 = jnp.bfloat16
I32 = jnp.int32
SPOTS = (-1.0, -0.5, 0.0, 0.5, 1.0)
NX = 4
NZ = 16
NB = 8
FRONT = 264
TW = 512
NT = (((1,), (1,)), ((), ()))
NN = (((1,), (0,)), ((), ()))


def iota(shape, axis):
    return lax.broadcasted_iota(I32, shape, axis)


def dot(a, b, dims):
    return lax.dot_general(a, b, dims, preferred_element_type=F32)


def hit(cond):
    return jnp.where(cond, 1.0, 0.0).astype(BF16)


def pick_kernel(donor_ref, elem_ref, coord_ref, owner_ref, w_ref, base_ref, ex_ref, w2_ref,
                table, hot, src, wf):
    block = lax.axis_index("obs")
    panel = lax.axis_index("panel")

    def table_step(tile, carry):
        lanes = pl.ds(pl.multiple_of(tile * 128, 128), 128)
        factors = []
        for direction in range(3):
            x = jnp.broadcast_to(coord_ref[direction:direction + 1, lanes], (8, 128))
            column = []
            for one in range(5):
                value = None
                for two in range(5):
                    if two != one:
                        term = (x - SPOTS[two]) * (1.0 / (SPOTS[one] - SPOTS[two]))
                        value = term if value is None else value * term
                column.append(value)
            factors.append(column)
        low = iota((8, 128), 0) < 4
        pairs = [[fa * fb for fb in factors[1]] for fa in factors[0]]
        node = lambda n: pairs[n // 25][(n // 5) % 5] * factors[2][n % 5]
        nodes = [node(n) for n in range(125)]
        for j in range(125):
            table[8 * j:8 * j + 8, lanes] = jnp.where(low, nodes[(2 * j) % 125], nodes[(2 * j + 1) % 125])
        return carry

    lax.fori_loop(0, 8, table_step, 0)

    hot[...] = hit(iota((128, 1024), 0) == elem_ref[...] - block * 128)

    def point_step(tile, carry):
        lanes = pl.ds(pl.multiple_of(tile * 256, 256), 256)
        for part in range(2):
            picked = dot(donor_ref[part * 2000:part * 2000 + 2000, :], hot[:, lanes], NN)
            for half in range(2):
                prod = picked[half * 1000:half * 1000 + 1000] * table[:, lanes]
                prod = prod.reshape(125, 8, 256)
                first = jnp.sum(prod[:62], axis=0)
                last = jnp.sum(prod[63:], axis=0)
                mid = prod[62]
                step = 2 * part + half
                even = first[:4] + first[4:] + mid[:4]
                odd = last[:4] + last[4:] + mid[4:]
                for side in range(2):
                    cols = slice(side * 128, side * 128 + 128)
                    src[2 * tile + side, pl.ds(step, 4, stride=4), :] = even[:, cols]
                    src[2 * tile + side, pl.ds(16 + step, 4, stride=4), :] = odd[:, cols]
        return carry

    lax.fori_loop(0, 4, point_step, 0)
    sources = jnp.concatenate([src[tile] for tile in range(8)], axis=1).astype(BF16).astype(F32)

    own = owner_ref[pl.ds(block, 1), :]
    member = iota((64, 1024), 0) == own
    member_f = jnp.where(member, 1.0, 0.0)
    member_b = member_f.astype(BF16)
    upper = hit(iota((128, 128), 0) < iota((128, 128), 1))
    ones = jnp.ones((128, 128), BF16)
    carry = jnp.zeros((64, 128), F32)
    ranks = []
    for tile in range(8):
        cols = slice(tile * 128, tile * 128 + 128)
        below = dot(member_b[:, cols], upper, NN) + carry
        ranks.append(jnp.sum(member_f[:, cols] * below, axis=0, keepdims=True))
        carry = carry + dot(member_b[:, cols], ones, NN)
    rank = jnp.concatenate(ranks, axis=1).astype(I32)

    spot = jnp.where(rank < 12, (own & 7) * 16 + rank, -1)
    place = hit(iota((128, 1024), 0) == spot)
    group = own >> 3
    left = jnp.concatenate([jnp.where(group == g, sources, 0.0).astype(BF16) for g in range(8)], axis=0)
    grouped = dot(left, place, NT)
    row = iota((32, 128), 0)
    lane = iota((32, 128), 1)
    for g in range(8):
        x = grouped[g * 32:g * 32 + 32]
        for k in range(3):
            r, l = 4 << k, 16 << k
            rbit, lbit = (row // r) & 1, (lane // l) & 1
            up = pltpu.roll(pltpu.roll(x, 32 - r, 0), l, 1)
            down = pltpu.roll(pltpu.roll(x, r, 0), 128 - l, 1)
            x = jnp.where(rbit == lbit, x, jnp.where(rbit == 0, up, down))
        base_ref[g * 32:g * 32 + 32, :] = x.astype(BF16)

    extra = rank - 12
    spot = jnp.where(rank >= 12, ((own >> 4) & 1) * 64 + (own & 15) * 4 + (extra & 3), -1)
    place = hit(iota((128, 1024), 0) == spot)
    group = (own >> 5) * 8 + (extra >> 2)
    half = iota((16, 128), 1) < 64
    for g in range(2):
        left = jnp.concatenate(
            [jnp.where(group == g * 8 + h, sources, 0.0).astype(BF16) for h in range(8)], axis=0)
        more = dot(left, place, NT)
        for h in range(8):
            r0, r1 = more[h * 32:h * 32 + 16], more[h * 32 + 16:h * 32 + 32]
            even = jnp.where(half, r0, pltpu.roll(r1, 64, 1))
            odd = jnp.where(half, pltpu.roll(r0, 64, 1), r1)
            at = ((2 * g) * 8 + h) * 16
            ex_ref[at:at + 16, :] = even.astype(BF16)
            at = ((2 * g + 1) * 8 + h) * 16
            ex_ref[at:at + 16, :] = odd.astype(BF16)

    wf[...] = w_ref[...].astype(F32)
    counts = jnp.sum(jnp.where(owner_ref[...] == panel, 1.0, 0.0), axis=1, keepdims=True)
    heavy = jnp.sum(jnp.where(counts > 28.0, iota((8, 1), 0).astype(F32), 0.0), axis=0, keepdims=True).astype(I32)
    slot_lane = iota((1, 512), 1)
    relay, quant, slot = slot_lane >> 6, (slot_lane >> 4) & 3, slot_lane & 15
    panel_at = jnp.where(slot < 12, 12 * relay + jnp.where(relay > heavy, 32, 0) + slot,
                         12 * heavy + 4 * relay + slot)
    target = quant * 128 + panel_at
    mover = hit(iota((512, 512), 0) == target)
    for k in range(4):
        rows = jnp.concatenate([wf[pl.ds(k * 4 + q, 128, stride=16), :].astype(BF16) for q in range(4)], axis=1)
        w2_ref[k * 128:k * 128 + 128, :] = dot(rows, mover, NN).astype(BF16)


def pick(donor, elem, coords, owner, weights):
    vmem = pl.BlockSpec(memory_space=pltpu.VMEM)
    return pl.pallas_call(
        pick_kernel,
        out_shape=(
            jax.ShapeDtypeStruct((256, 128), BF16),
            jax.ShapeDtypeStruct((512, 128), BF16),
            jax.ShapeDtypeStruct((512, 512), BF16),
        ),
        in_specs=[vmem] * 5,
        out_specs=(vmem, vmem, vmem),
        scratch_shapes=[
            pltpu.VMEM((1000, 1024), F32),
            pltpu.VMEM((128, 1024), BF16),
            pltpu.VMEM((8, 32, 128), F32),
            pltpu.VMEM((2048, 128), F32),
        ],
        compiler_params=pltpu.CompilerParams(vmem_limit_bytes=48 * 2**20),
    )(donor, elem, coords, owner, weights)


def mix_pair(a, b, low):
    return jnp.where(low, a, pltpu.roll(b, 4, 0)), jnp.where(low, pltpu.roll(a, 4, 0), b)


def move_kernel(base_ref, ex_ref, w2_ref, off_ref, out_ref,
                base_in, ex_in, msg, held, wide, part, part_b, part_in, line, line_in,
                base_s, base_r, ex_s, ex_r, z_s, z_r, o_s, o_r, px_s, px_r, pz_s, pz_r, own_sem):
    panel = lax.axis_index("panel")
    b = lax.axis_index("obs")
    x = panel // NZ
    z = panel % NZ
    me = x * NB + b

    def at(px, pz, pb):
        return {"panel": px * NZ + pz, "obs": pb}

    def remote(src, dst, send, recv, device):
        return pltpu.make_async_remote_copy(
            src_ref=src, dst_ref=dst, send_sem=send, recv_sem=recv,
            device_id=device, device_id_type=pl.DeviceIdType.MESH)

    barrier = pltpu.get_barrier_semaphore()

    def greet(i, c):
        slot = (me + i) % 32
        pl.semaphore_signal(barrier, inc=1, device_id=at(slot // NB, z, slot % NB),
                            device_id_type=pl.DeviceIdType.MESH)
        return c

    def greet_z(i, c):
        pl.semaphore_signal(barrier, inc=1, device_id=at(x, (z + i) % NZ, b),
                            device_id_type=pl.DeviceIdType.MESH)
        return c

    lax.fori_loop(1, 32, greet, 0)
    lax.fori_loop(1, NZ, greet_z, 0)
    pl.semaphore_wait(barrier, 46)

    def base_copy(px, source):
        return remote(base_ref.at[pl.ds(px * 64, 64)], base_in.at[source], base_s.at[px], base_r.at[source],
                      at(px, z, b))

    def ex_copy(slot, source):
        return remote(ex_ref.at[pl.ds(slot * 16, 16)], ex_in.at[source], ex_s.at[slot], ex_r.at[source],
                      at(slot // NB, z, slot % NB))

    def base_start(i, c):
        base_copy((x + i) % NX, x).start()
        return c

    def ex_start(i, c):
        ex_copy((me + i) % 32, me).start()
        return c

    lax.fori_loop(1, NX, base_start, 0)
    lax.fori_loop(1, 32, ex_start, 0)
    own_base = pltpu.make_async_copy(base_ref.at[pl.ds(x * 64, 64)], base_in.at[x], own_sem.at[0])
    own_ex = pltpu.make_async_copy(ex_ref.at[pl.ds(me * 16, 16)], ex_in.at[me], own_sem.at[1])
    own_base.start()
    own_ex.start()
    wide[:, 0:FRONT, :] = jnp.zeros((4, FRONT, 128), F32)
    own_base.wait()
    own_ex.wait()

    def base_wait(i, c):
        base_copy((x + i) % NX, (x + i) % NX).wait_recv()
        return c

    def ex_wait(i, c):
        ex_copy((me + i) % 32, (me + i) % 32).wait_recv()
        return c

    lax.fori_loop(1, NX, base_wait, 0)
    lax.fori_loop(1, 32, ex_wait, 0)

    low = iota((8, 128), 0) < 4
    lane = iota((8, 128), 1)
    sums = []
    for px in range(NX):
        total = ex_in[px * NB].astype(F32)
        for pb in range(1, NB):
            total = total + ex_in[px * NB + pb].astype(F32)
        sums.append(total)
    quants = []
    for v in range(2):
        rows = slice(v * 8, v * 8 + 8)
        e01, o01 = mix_pair(sums[0][rows], sums[1][rows], low)
        e23, o23 = mix_pair(sums[2][rows], sums[3][rows], low)
        quants += [(e01, e23), (o01, o23)]
    bases = [base_in[px].astype(F32) for px in range(NX)]
    masks = [((lane & 63) >= 16 * q + 12) & ((lane & 63) < 16 * q + 16) for q in range(4)]
    for v in range(8):
        rows = slice(v * 8, v * 8 + 8)
        e01, o01 = mix_pair(bases[0][rows], bases[1][rows], low)
        e23, o23 = mix_pair(bases[2][rows], bases[3][rows], low)
        for pz, halves in ((2 * v, (e01, e23)), (2 * v + 1, (o01, o23))):
            done = []
            for h in range(2):
                value = halves[h]
                for q in range(4):
                    shift = (16 * q + 12 - 4 * pz) % 128
                    value = jnp.where(masks[q], pltpu.roll(quants[q][h], shift, 1), value)
                done.append(value)
            msg[pz] = jnp.concatenate(done, axis=0).astype(BF16)

    def z_copy(pz, source):
        return remote(msg.at[pz], held.at[b, pl.ds(source * 16, 16)], z_s.at[pz], z_r.at[source], at(x, pz, b))

    def z_start(i, c):
        z_copy((z + i) % NZ, z).start()
        return c

    def z_wait(i, c):
        z_copy((z + i) % NZ, (z + i) % NZ).wait_recv()
        return c

    lax.fori_loop(1, NZ, z_start, 0)
    own_z = pltpu.make_async_copy(msg.at[z], held.at[b, pl.ds(z * 16, 16)], own_sem.at[0])
    own_z.start()
    own_z.wait()
    lax.fori_loop(1, NZ, z_wait, 0)

    def o_copy(pb, source):
        return remote(held.at[source], held.at[source], o_s.at[pb], o_r.at[source], at(x, z, pb))

    def o_start(i, c):
        o_copy((b + i) % NB, b).start()
        return c

    def o_wait(i, c):
        o_copy((b + i) % NB, (b + i) % NB).wait_recv()
        return c

    lax.fori_loop(1, NB, o_start, 0)
    lax.fori_loop(1, NB, o_wait, 0)

    low_wide = iota((8, 512), 0) < 4
    for parity in range(2):
        cols = slice(parity * 64, parity * 64 + 64)
        left = jnp.concatenate([held[pb][:, cols] for pb in range(NB)], axis=1)
        y = dot(left, w2_ref[...], NT)
        for xp in range(2):
            evens, odds = [], []
            for v in range(8):
                first = y[v * 32 + xp * 8:v * 32 + xp * 8 + 8]
                second = y[v * 32 + 16 + xp * 8:v * 32 + 16 + xp * 8 + 8]
                even, odd = mix_pair(first, second, low_wide)
                evens.append(even)
                odds.append(odd)
            even, odd = jnp.concatenate(evens, axis=0), jnp.concatenate(odds, axis=0)
            for k in range(4):
                cols = slice(k * 128, k * 128 + 128)
                wide[k, pl.ds(FRONT + 256 * xp + parity, 64, stride=2), :] = even[:, cols]
                wide[k, pl.ds(FRONT + 256 * xp + 128 + parity, 64, stride=2), :] = odd[:, cols]
    delay = off_ref[0, 0]
    total = wide[0, pl.ds(FRONT - delay, TW), :]
    for k in range(1, 4):
        total = total + wide[k, pl.ds(FRONT - delay - k, TW), :]
    part[...] = total
    part_b[...] = total.astype(BF16).reshape(NX, 128, 128)

    def px_copy(px, source):
        return remote(part_b.at[px], part_in.at[source], px_s.at[px], px_r.at[source], at(px, z, b))

    def px_start(i, c):
        px_copy((x + i) % NX, x).start()
        return c

    lax.fori_loop(1, NX, px_start, 0)
    acc = part[pl.ds(x * 128, 128), :]
    for i in range(1, NX):
        source = (x + i) % NX
        px_copy(source, source).wait_recv()
        acc = acc + part_in[source].astype(F32)
    line[...] = acc

    def pz_copy(pz, source):
        return remote(line.at[pl.ds(pz * 8, 8)], line_in.at[source], pz_s.at[pz], pz_r.at[source], at(x, pz, b))

    def pz_start(i, c):
        pz_copy((z + i) % NZ, z).start()
        return c

    lax.fori_loop(1, NZ, pz_start, 0)
    acc = line[pl.ds(z * 8, 8), :]
    for i in range(1, NZ):
        source = (z + i) % NZ
        pz_copy(source, source).wait_recv()
        acc = acc + line_in[source]
    out_ref[...] = acc

    def base_end(i, c):
        base_copy((x + i) % NX, x).wait_send()
        px_copy((x + i) % NX, x).wait_send()
        return c

    def ex_end(i, c):
        ex_copy((me + i) % 32, me).wait_send()
        return c

    def z_end(i, c):
        z_copy((z + i) % NZ, z).wait_send()
        pz_copy((z + i) % NZ, z).wait_send()
        return c

    def o_end(i, c):
        o_copy((b + i) % NB, b).wait_send()
        return c

    lax.fori_loop(1, NX, base_end, 0)
    lax.fori_loop(1, 32, ex_end, 0)
    lax.fori_loop(1, NZ, z_end, 0)
    lax.fori_loop(1, NB, o_end, 0)


def move(base, ex, w2, offsets):
    vmem = pl.BlockSpec(memory_space=pltpu.VMEM)
    dma = pltpu.SemaphoreType.DMA
    return pl.pallas_call(
        move_kernel,
        out_shape=jax.ShapeDtypeStruct((8, 128), F32),
        in_specs=[vmem, vmem, vmem, pl.BlockSpec(memory_space=pltpu.SMEM)],
        out_specs=vmem,
        scratch_shapes=[
            pltpu.VMEM((NX, 64, 128), BF16),
            pltpu.VMEM((NX * NB, 16, 128), BF16),
            pltpu.VMEM((NZ, 16, 128), BF16),
            pltpu.VMEM((NB, 256, 128), BF16),
            pltpu.VMEM((4, FRONT + TW, 128), F32),
            pltpu.VMEM((TW, 128), F32),
            pltpu.VMEM((NX, 128, 128), BF16),
            pltpu.VMEM((NX, 128, 128), BF16),
            pltpu.VMEM((128, 128), F32),
            pltpu.VMEM((NZ, 8, 128), F32),
            dma((NX,)), dma((NX,)), dma((32,)), dma((32,)), dma((NZ,)), dma((NZ,)),
            dma((NB,)), dma((NB,)), dma((NX,)), dma((NX,)), dma((NZ,)), dma((NZ,)), dma((2,)),
        ],
        compiler_params=pltpu.CompilerParams(
            collective_id=0, has_side_effects=True, vmem_limit_bytes=48 * 2**20),
    )(base, ex, w2, offsets)


def body(donor, donor_elem, local_coords, owner, weights, offsets):
    base, ex, w2 = pick(
        donor.reshape(4000, 128),
        donor_elem.reshape(1, 1024),
        local_coords,
        owner.reshape(8, 1024),
        weights.reshape(2048, 128),
    )
    return move(base, ex, w2, offsets)


def solution(mesh):
    return jax.shard_map(
        body,
        mesh=mesh,
        in_specs=(
            P("panel", None, None, "obs"),
            P("obs"),
            P(None, "obs"),
            P(),
            P("obs", None, None, "panel"),
            P("obs", "panel"),
        ),
        out_specs=P("panel", "obs"),
        check_vma=False,
    )
```

time: 637 us -> 64.8 us (0.10); the launches traced: 627 us -> 64.5 us
  waiting for transfers between devices: 274 us -> 0 us
  other arithmetic: 157 us -> 0 us
  local copies, waits for them, and re-layouts: 146 us -> 4.31 us
  Pallas kernels: 0 us -> 59.5 us
  blocking collectives: 19.8 us -> 0 us
  between operations: 14.8 us -> 0.69 us
  starting transfers between devices: 13.7 us -> 0 us
    unnamed x2 -> x0, waiting for transfers between devices: 245 us -> none
    reduce_sum x8 -> x0, other arithmetic: 116 us -> none  [one_time(): return jnp.sum(node_table[:, None, :] * values, axis=0).astype(jnp.bfloat16)]
    gather x9 -> x0, local copies, waits for them, and re-layouts: 88.2 us -> none  [the longest x1 59.6 us: body(): outgoing = jnp.take(everything, order, axis=2)]
    pallas_call x0 -> x2, Pallas kernels: none -> 59.5 us  [the longest x1 54.6 us: move(): pl.pallas_call(move_kernel, out_shape=jax.ShapeDtypeStruct((8, 128), F32)...]
    unnamed x1 -> x0, other arithmetic: 30.9 us -> none
    all_to_all x1 -> x0, waiting for transfers between devices: 29.2 us -> none  [body(): lax.all_to_all(outgoing, 'panel', split_axis=2, concat_axis=0, tiled=True)]
    unnamed x6 -> x9, local copies, waits for them, and re-layouts: 24.6 us -> 3.53 us
    all_gather x1 -> x0, blocking collectives: 19.8 us -> none  [body(): everything = lax.all_gather(local_sources, 'obs', axis=2, tiled=True)]
  transfers between devices with their start and end apart: 2 -> 0, of which waited for: 2 -> 0; matrix products, arithmetic and copies ran while one was open for 0% -> 0% of each run, Pallas kernels for 0% -> 0%
where the time goes in v1:
time: 64.8 us; the launch traced here: 64.5 us
  Pallas kernels  59.5 us (92%)
  local copies, waits for them, and re-layouts  4.31 us (7%)
  between operations  0.69 us (1%)
    pallas_call x1, Pallas kernels, move(): pl.pallas_call(move_kernel, out_shape=jax.ShapeDtypeStruct((8, 128), F32)...  54.6 us
    pallas_call x1, Pallas kernels, pick(): pl.pallas_call(pick_kernel, out_shape=(jax.ShapeDtypeStruct((256, 128), B...  4.88 us
    unnamed x9, local copies, waits for them, and re-layouts  3.53 us

profile of v1, /device:TPU:1, one launch (start us, length us, event | category | flops | bytes accessed | tf_op | source)
XLA Modules:
  0.0 64.5 jit_solution(13387274255687532024)
XLA Ops:
  0.0 0.0 copy-start.2
  0.0 0.8 %reshape.14.owner_ref = s32[8,1024]{1,0:T(8,128)S(1)} reshape(s32[8192]{0:T(1024)} %param.9) | data formatting | bytes 65536 | tf_op jit(solution)/shard_map/reshape | solution.py:420
  0.8 0.0 copy-start.3
  0.8 0.0 copy-done.2
  0.8 0.7 %copy-done.3 = s32[1024]{0:T(1024)S(1)} copy-done((s32[1024]{0:T(1024)S(1)}, s32[1024]{0:T(1024)}, u32[]{:S(2)}) %copy-start.3) | copy-done | bytes 4120
  1.5 0.0 copy-start
  1.5 1.2 %copy-done = bf16[8,125,4,128]{3,2,1,0:T(4,128)(2,1)S(1)} copy-done((bf16[8,125,4,128]{3,2,1,0:T(4,128)(2,1)S(1)}, bf16[8,125,4,128]{3,2,1,0:T(4,128)(2,1)}, u32[]{:S(2)}) %copy-start) | copy-done | bytes 1024024
  2.7 0.0 copy-start.1
  2.7 1.0 %copy-done.1 = bf16[128,4,4,128]{3,2,1,0:T(4,128)(2,1)S(1)} copy-done((bf16[128,4,4,128]{3,2,1,0:T(4,128)(2,1)S(1)}, bf16[128,4,4,128]{3,2,1,0:T(4,128)(2,1)}, u32[]{:S(2)}) %copy-start.1) | copy-done | bytes 524312
  3.7 4.9 %shard_map.64 = (bf16[256,128]{1,0:T(8,128)(2,1)S(1)}, bf16[512,128]{1,0:T(8,128)(2,1)S(1)}, bf16[512,512]{1,0:T(8,128)(2,1)S(1)}) custom-call(bf16[4000,128]{1,0:T(8,128)(2,1)S(1)} %bitcast.3, s32[1,1024]{1,0:T(1,128)S(1)} %bitcast.5, f32[3,1024]{1,0:T(4,128)S(1)} %copy-done.2, s32[8,1024]{1,0:T(8,128)S(1)} %reshape.14.owner_ref, bf16[2048,128]{1,0:T(8,128)(2,1)S(1)} %bitcast.4), custom_call_target="tpu_custom_call" | custom-call | tf_op jit(solution)/shard_map/pallas_call | solution.py:154
  9.3 54.6 %shard_map.65 = f32[8,128]{1,0:T(8,128)S(1)} custom-call(bf16[256,128]{1,0:T(8,128)(2,1)S(1)} %get-tuple-element.8.base_ref, bf16[512,128]{1,0:T(8,128)(2,1)S(1)} %get-tuple-element.9.ex_ref, bf16[512,512]{1,0:T(8,128)(2,1)S(1)} %get-tuple-element.10.w2_ref, s32[1,1]{1,0:T(1,128)S(6)} %copy.8.off_ref), custom_call_target="tpu_custom_call" | custom-call | tf_op jit(solution)/shard_map/pallas_call | solution.py:391
  63.9 0.6 copy.9
Async XLA Ops:
  0.0 0.8 %copy-start.2 = (f32[3,1024]{1,0:T(4,128)S(1)}, f32[3,1024]{1,0:T(4,128)}, u32[]{:S(2)}) copy-start(f32[3,1024]{1,0:T(4,128)} %coord_ref.1) | copy-start | bytes 36868
  0.8 0.7 %copy-start.3 = (s32[1024]{0:T(1024)S(1)}, s32[1024]{0:T(1024)}, u32[]{:S(2)}) copy-start(s32[1024]{0:T(1024)} %param.7) | copy-start | bytes 12292
  1.5 1.2 %copy-start = (bf16[8,125,4,128]{3,2,1,0:T(4,128)(2,1)S(1)}, bf16[8,125,4,128]{3,2,1,0:T(4,128)(2,1)}, u32[]{:S(2)}) copy-start(bf16[8,125,4,128]{3,2,1,0:T(4,128)(2,1)} %param.6) | copy-start | bytes 3072004
  2.7 1.0 %copy-start.1 = (bf16[128,4,4,128]{3,2,1,0:T(4,128)(2,1)S(1)}, bf16[128,4,4,128]{3,2,1,0:T(4,128)(2,1)}, u32[]{:S(2)}) copy-start(bf16[128,4,4,128]{3,2,1,0:T(4,128)(2,1)} %param.10) | copy-start | bytes 1572868

commit v2 on v1

v2 whole, which is shorter than its diff:
```python
import jax
import jax.numpy as jnp
from jax import lax
from jax.experimental import pallas as pl
from jax.experimental.pallas import tpu as pltpu
from jax.sharding import PartitionSpec as P

F32 = jnp.float32
BF16 = jnp.bfloat16
I32 = jnp.int32
SPOTS = (-1.0, -0.5, 0.0, 0.5, 1.0)
NX = 4
NZ = 16
NB = 8
FRONT = 264
TW = 512
NT = (((1,), (1,)), ((), ()))
NN = (((1,), (0,)), ((), ()))
MESH = pl.DeviceIdType.MESH
GROUPS = ((0, 112), (112, 96), (208, 48))
GROUP_ENDS = (7, 13, 16)
OBS_ORDER = (4, 3, 5, 2, 6, 7, 1)


def iota(shape, axis):
    return lax.broadcasted_iota(I32, shape, axis)


def dot(a, b, dims):
    return lax.dot_general(a, b, dims, preferred_element_type=F32)


def hit(cond):
    return jnp.where(cond, 1.0, 0.0).astype(BF16)


def flat_row(tiles):
    return jnp.concatenate([tiles[t:t + 1] for t in range(8)], axis=1)


def mix_pair(a, b, low):
    return jnp.where(low, a, pltpu.roll(b, 4, 0)), jnp.where(low, pltpu.roll(a, 4, 0), b)


def fill_table(coord_ref, table):
    def table_step(tile, carry):
        lanes = pl.ds(pl.multiple_of(tile * 128, 128), 128)
        factors = []
        for direction in range(3):
            x = jnp.broadcast_to(coord_ref[direction:direction + 1, lanes], (8, 128))
            column = []
            for one in range(5):
                value = None
                for two in range(5):
                    if two != one:
                        term = (x - SPOTS[two]) * (1.0 / (SPOTS[one] - SPOTS[two]))
                        value = term if value is None else value * term
                column.append(value)
            factors.append(column)
        low = iota((8, 128), 0) < 4
        pairs = [[fa * fb for fb in factors[1]] for fa in factors[0]]
        nodes = [pairs[n // 25][(n // 5) % 5] * factors[2][n % 5] for n in range(125)]
        for j in range(125):
            table[8 * j:8 * j + 8, lanes] = jnp.where(low, nodes[(2 * j) % 125], nodes[(2 * j + 1) % 125])
        return carry

    lax.fori_loop(0, 8, table_step, 0)


def fill_sources(donor, hot, table, src):
    def point_step(tile, carry):
        lanes = pl.ds(pl.multiple_of(tile * 256, 256), 256)
        for part in range(2):
            picked = dot(donor[part * 2000:part * 2000 + 2000, :], hot[:, lanes], NN)
            for half in range(2):
                prod = picked[half * 1000:half * 1000 + 1000] * table[:, lanes]
                prod = prod.reshape(125, 8, 256)
                first = jnp.sum(prod[:62], axis=0)
                last = jnp.sum(prod[63:], axis=0)
                mid = prod[62]
                step = 16 * part + 2 * half
                even = first[:4] + first[4:] + mid[:4]
                odd = last[:4] + last[4:] + mid[4:]
                for side in range(2):
                    cols = slice(side * 128, side * 128 + 128)
                    src[2 * tile + side, pl.ds(step, 4, stride=4), :] = even[:, cols]
                    src[2 * tile + side, pl.ds(step + 1, 4, stride=4), :] = odd[:, cols]
        return carry

    lax.fori_loop(0, 4, point_step, 0)


def rank_points(own):
    member = iota((64, 1024), 0) == own
    member_f = jnp.where(member, 1.0, 0.0)
    member_b = member_f.astype(BF16)
    upper = hit(iota((128, 128), 0) < iota((128, 128), 1))
    ones = jnp.ones((128, 128), BF16)
    carry = jnp.zeros((64, 128), F32)
    ranks = []
    for tile in range(8):
        cols = slice(tile * 128, tile * 128 + 128)
        below = dot(member_b[:, cols], upper, NN) + carry
        ranks.append(jnp.sum(member_f[:, cols] * below, axis=0, keepdims=True))
        carry = carry + dot(member_b[:, cols], ones, NN)
    return jnp.concatenate(ranks, axis=1).astype(I32)


def group_base(sources, own, rank, base_ref):
    spot = jnp.where(rank < 12, (own & 7) * 16 + rank, -1)
    place = hit(iota((128, 1024), 0) == spot)
    group = own >> 3
    left = jnp.concatenate([jnp.where(group == g, sources, 0.0).astype(BF16) for g in range(8)], axis=0)
    grouped = dot(left, place, NT)
    row = iota((32, 128), 0)
    lane = iota((32, 128), 1)
    for g in range(8):
        x = grouped[g * 32:g * 32 + 32]
        for k in range(3):
            r, l = 4 << k, 16 << k
            rbit, lbit = (row >> (2 + k)) & 1, (lane >> (4 + k)) & 1
            up = pltpu.roll(pltpu.roll(x, 32 - r, 0), l, 1)
            down = pltpu.roll(pltpu.roll(x, r, 0), 128 - l, 1)
            x = jnp.where(rbit == lbit, x, jnp.where(rbit == 0, up, down))
        base_ref[g * 32:g * 32 + 32, :] = x.astype(BF16)


def group_extra(sources, own, rank, ex_ref):
    extra = rank - 12
    spot = jnp.where(rank >= 12, ((own >> 4) & 1) * 64 + (own & 15) * 4 + (extra & 3), -1)
    place = hit(iota((128, 1024), 0) == spot)
    group = (own >> 5) * 8 + (extra >> 2)
    half = iota((16, 128), 1) < 64
    for g in range(2):
        left = jnp.concatenate(
            [jnp.where(group == g * 8 + h, sources, 0.0).astype(BF16) for h in range(8)], axis=0)
        more = dot(left, place, NT)
        for h in range(8):
            r0, r1 = more[h * 32:h * 32 + 16], more[h * 32 + 16:h * 32 + 32]
            even = jnp.where(half, r0, pltpu.roll(r1, 64, 1))
            odd = jnp.where(half, pltpu.roll(r0, 64, 1), r1)
            at = ((2 * g) * 8 + h) * 16
            ex_ref[at:at + 16, :] = even.astype(BF16)
            at = ((2 * g + 1) * 8 + h) * 16
            ex_ref[at:at + 16, :] = odd.astype(BF16)


def order_weights(w_ref, owner_ref, panel, wf, w2_ref):
    wf[...] = w_ref[...].astype(F32)
    same = jnp.where(owner_ref[...] == panel, 1.0, 0.0)
    heavy = jnp.zeros((1, 1), F32)
    for block in range(1, 8):
        count = jnp.sum(jnp.sum(same[block * 8:block * 8 + 8], axis=0, keepdims=True), axis=1, keepdims=True)
        heavy = heavy + jnp.where(count > 28.0, float(block), 0.0)
    heavy = heavy.astype(I32)
    slot_lane = iota((1, 512), 1)
    relay, quant, slot = slot_lane >> 6, (slot_lane >> 4) & 3, slot_lane & 15
    panel_at = jnp.where(slot < 12, 12 * relay + jnp.where(relay > heavy, 32, 0) + slot,
                         12 * heavy + 4 * relay + slot)
    mover = hit(iota((512, 512), 0) == quant * 128 + panel_at)
    for k in range(4):
        rows = jnp.concatenate([wf[pl.ds(k * 4 + q, 128, stride=16), :].astype(BF16) for q in range(4)], axis=1)
        w2_ref[k * 128:k * 128 + 128, :] = dot(rows, mover, NN).astype(BF16)


def fill_messages(base_in, ex_in, msg):
    low = iota((8, 128), 0) < 4
    lane = iota((8, 128), 1)
    sums = []
    for px in range(NX):
        total = ex_in[px * NB].astype(F32)
        for pb in range(1, NB):
            total = total + ex_in[px * NB + pb].astype(F32)
        sums.append(total)
    quants = []
    for v in range(2):
        rows = slice(v * 8, v * 8 + 8)
        e01, o01 = mix_pair(sums[0][rows], sums[1][rows], low)
        e23, o23 = mix_pair(sums[2][rows], sums[3][rows], low)
        quants += [(e01, e23), (o01, o23)]
    bases = [base_in[px].astype(F32) for px in range(NX)]
    masks = [((lane & 63) >= 16 * q + 12) & ((lane & 63) < 16 * q + 16) for q in range(4)]
    for v in range(8):
        rows = slice(v * 8, v * 8 + 8)
        e01, o01 = mix_pair(bases[0][rows], bases[1][rows], low)
        e23, o23 = mix_pair(bases[2][rows], bases[3][rows], low)
        for pz, halves in ((2 * v, (e01, e23)), (2 * v + 1, (o01, o23))):
            done = []
            for h in range(2):
                value = halves[h]
                for q in range(4):
                    shift = (16 * q + 12 - 4 * pz) % 128
                    value = jnp.where(masks[q], pltpu.roll(quants[q][h], shift, 1), value)
                done.append(value)
            msg[pz] = jnp.concatenate(done, axis=0).astype(BF16)


def kernel(donor_hbm, elem_ref, coord_ref, owner_ref, w_hbm, off_ref, out_ref,
           donor, weights, table, hot, src, wf, w2, base_out, ex_out,
           base_in, ex_in, msg, held, wide, part, part_b, part_in, line, line_in,
           base_s, base_r, ex_s, ex_r, z_s, z_r, o_s, o_r, px_s, px_r, pz_s, pz_r, own_sem):
    panel = lax.axis_index("panel")
    b = lax.axis_index("obs")
    x = panel // NZ
    z = panel % NZ
    me = x * NB + b

    def at(px, pz, pb):
        return {"panel": px * NZ + pz, "obs": pb}

    def remote(src_ref, dst_ref, send, recv, device):
        return pltpu.make_async_remote_copy(
            src_ref=src_ref, dst_ref=dst_ref, send_sem=send, recv_sem=recv,
            device_id=device, device_id_type=MESH)

    donor_copy = pltpu.make_async_copy(donor_hbm, donor, own_sem.at[0])
    weight_copy = pltpu.make_async_copy(w_hbm, weights, own_sem.at[1])
    donor_copy.start()
    weight_copy.start()
    barrier = pltpu.get_barrier_semaphore()

    def greet(i, c):
        slot = (me + i) % 32
        pl.semaphore_signal(barrier, inc=1, device_id=at(slot // NB, z, slot % NB), device_id_type=MESH)
        return c

    def greet_z(i, c):
        pl.semaphore_signal(barrier, inc=1, device_id=at(x, (z + i) % NZ, b), device_id_type=MESH)
        return c

    lax.fori_loop(1, NZ, greet_z, 0)
    lax.fori_loop(1, 32, greet, 0)

    fill_table(coord_ref, table)
    hot[...] = hit(iota((128, 1024), 0) == elem_ref[...] - b * 128)
    own = flat_row(owner_ref[pl.ds(b * 8, 8), :])
    rank = rank_points(own)
    donor_copy.wait()
    fill_sources(donor, hot, table, src)
    sources = jnp.concatenate([src[tile] for tile in range(8)], axis=1).astype(BF16).astype(F32)
    group_extra(sources, own, rank, ex_out)
    group_base(sources, own, rank, base_out)
    pl.semaphore_wait(barrier, 46)

    def base_copy(px, source):
        return remote(base_out.at[pl.ds(px * 64, 64)], base_in.at[source], base_s.at[px], base_r.at[source],
                      at(px, z, b))

    def ex_copy(slot, source):
        return remote(ex_out.at[pl.ds(slot * 16, 16)], ex_in.at[source], ex_s.at[slot], ex_r.at[source],
                      at(slot // NB, z, slot % NB))

    def ex_start(j, c):
        ex_copy((me + 12 + j + j // 20) % 32, me).start()
        return c

    for i in (2, 1, 3):
        base_copy((x + i) % NX, x).start()
    lax.fori_loop(0, 31, ex_start, 0)
    weight_copy.wait()
    own_base = pltpu.make_async_copy(base_out.at[pl.ds(x * 64, 64)], base_in.at[x], own_sem.at[0])
    own_ex = pltpu.make_async_copy(ex_out.at[pl.ds(me * 16, 16)], ex_in.at[me], own_sem.at[1])
    own_base.start()
    own_ex.start()
    wide[:, 0:FRONT, :] = jnp.zeros((4, FRONT, 128), F32)
    order_weights(weights, owner_ref, panel, wf, w2)
    own_base.wait()
    own_ex.wait()

    def ex_wait(i, c):
        ex_copy((me + i) % 32, (me + i) % 32).wait_recv()
        return c

    for i in (1, 3, 2):
        base_copy((x + i) % NX, (x + i) % NX).wait_recv()
    lax.fori_loop(1, 32, ex_wait, 0)
    fill_messages(base_in, ex_in, msg)

    def away(i):
        h = (i + 1) // 2
        return h + (1 - i % 2) * (NZ - 2 * h)

    def z_copy(i):
        pz = (z + NZ - away(i)) % NZ
        return remote(msg.at[pz], held.at[b, pl.ds(i * 16, 16)], z_s.at[i], z_r.at[i], at(x, pz, b))

    def z_start(i, c):
        z_copy(NZ - i).start()
        return c

    def z_wait(i, c):
        z_copy(i).wait_recv()
        return c

    lax.fori_loop(1, NZ, z_start, 0)
    own_z = pltpu.make_async_copy(msg.at[z], held.at[b, pl.ds(0, 16)], own_sem.at[0])
    own_z.start()
    own_z.wait()

    def o_copy(g, pb, source):
        rows = pl.ds(*GROUPS[g])
        return remote(held.at[source, rows], held.at[source, rows], o_s.at[g * NB + pb], o_r.at[g * NB + source],
                      at(x, z, pb))

    begin = 1
    for g in range(3):
        lax.fori_loop(begin, GROUP_ENDS[g], z_wait, 0)
        begin = GROUP_ENDS[g]
        for i in OBS_ORDER:
            o_copy(g, (b + i) % NB, b).start()
    for g in range(3):
        for i in range(1, NB):
            o_copy(g, (b + i) % NB, (b + i) % NB).wait_recv()

    low_wide = iota((8, 512), 0) < 4
    halves = []
    for side in range(2):
        cols = slice(side * 64, side * 64 + 64)
        left = jnp.concatenate([held[pb][:, cols] for pb in range(NB)], axis=1)
        halves.append(dot(left, w2[...], NT))
    for i in range(NZ):
        time = FRONT + 8 * ((z + away(i)) % NZ)
        for xp in range(2):
            rows = slice(i * 16 + xp * 8, i * 16 + xp * 8 + 8)
            pair = mix_pair(halves[0][rows], halves[1][rows], low_wide)
            for side in range(2):
                start = pl.multiple_of(time + 128 * (2 * xp + side), 8)
                for k in range(4):
                    wide[k, pl.ds(start, 8), :] = pair[side][:, k * 128:k * 128 + 128]
    delay = off_ref[0, 0]
    total = wide[0, pl.ds(FRONT - delay, TW), :]
    for k in range(1, 4):
        total = total + wide[k, pl.ds(FRONT - delay - k, TW), :]
    part[...] = total
    part_b[...] = total.astype(BF16).reshape(NX, 128, 128)

    def px_copy(i):
        px = (x + NX - i) % NX
        return remote(part_b.at[px], part_in.at[i], px_s.at[i], px_r.at[i], at(px, z, b))

    for i in (2, 1, 3):
        px_copy(i).start()
    acc = part[pl.ds(pl.multiple_of(x * 128, 128), 128), :]
    for i in (1, 3, 2):
        px_copy(i).wait_recv()
        acc = acc + part_in[i].astype(F32)
    line[...] = acc

    def pz_copy(i):
        pz = (z + NZ - away(i)) % NZ
        return remote(line.at[pl.ds(pz * 8, 8)], line_in.at[i], pz_s.at[i], pz_r.at[i], at(x, pz, b))

    def pz_start(i, c):
        pz_copy(NZ - i).start()
        return c

    def pz_wait(i, c):
        pz_copy(i).wait_recv()
        return c

    lax.fori_loop(1, NZ, pz_start, 0)

    def ex_end(i, c):
        ex_copy((me + i) % 32, me).wait_send()
        return c

    def z_end(i, c):
        z_copy(i).wait_send()
        return c

    def pz_end(i, c):
        pz_copy(i).wait_send()
        return c

    for i in range(1, NX):
        base_copy((x + i) % NX, x).wait_send()
        px_copy(i).wait_send()
    lax.fori_loop(1, 32, ex_end, 0)
    lax.fori_loop(1, NZ, z_end, 0)
    for g in range(3):
        for i in range(1, NB):
            o_copy(g, (b + i) % NB, b).wait_send()
    lax.fori_loop(1, NZ, pz_end, 0)

    acc = line[pl.ds(pl.multiple_of(z * 8, 8), 8), :]
    lax.fori_loop(1, NZ, pz_wait, 0)
    for i in range(1, NZ):
        acc = acc + line_in[i]
    out_ref[...] = acc


def body(donor, donor_elem, local_coords, owner, weights, offsets):
    vmem = pl.BlockSpec(memory_space=pltpu.VMEM)
    anywhere = pl.BlockSpec(memory_space=pl.ANY)
    dma = pltpu.SemaphoreType.DMA
    return pl.pallas_call(
        kernel,
        out_shape=jax.ShapeDtypeStruct((8, 128), F32),
        in_specs=[anywhere, vmem, vmem, vmem, anywhere, pl.BlockSpec(memory_space=pltpu.SMEM)],
        out_specs=vmem,
        scratch_shapes=[
            pltpu.VMEM((4000, 128), BF16),
            pltpu.VMEM((2048, 128), BF16),
            pltpu.VMEM((1000, 1024), F32),
            pltpu.VMEM((128, 1024), BF16),
            pltpu.VMEM((8, 32, 128), F32),
            pltpu.VMEM((2048, 128), F32),
            pltpu.VMEM((512, 512), BF16),
            pltpu.VMEM((256, 128), BF16),
            pltpu.VMEM((512, 128), BF16),
            pltpu.VMEM((NX, 64, 128), BF16),
            pltpu.VMEM((NX * NB, 16, 128), BF16),
            pltpu.VMEM((NZ, 16, 128), BF16),
            pltpu.VMEM((NB, 256, 128), BF16),
            pltpu.VMEM((4, FRONT + TW, 128), F32),
            pltpu.VMEM((TW, 128), F32),
            pltpu.VMEM((NX, 128, 128), BF16),
            pltpu.VMEM((NX, 128, 128), BF16),
            pltpu.VMEM((128, 128), F32),
            pltpu.VMEM((NZ, 8, 128), F32),
            dma((NX,)), dma((NX,)), dma((32,)), dma((32,)), dma((NZ,)), dma((NZ,)),
            dma((3 * NB,)), dma((3 * NB,)), dma((NX,)), dma((NX,)), dma((NZ,)), dma((NZ,)), dma((2,)),
        ],
        compiler_params=pltpu.CompilerParams(
            collective_id=0, has_side_effects=True, vmem_limit_bytes=60 * 2**20),
    )(
        donor.reshape(4000, 128),
        donor_elem.reshape(1, 1024),
        local_coords,
        owner.reshape(64, 128),
        weights.reshape(2048, 128),
        offsets,
    )


def solution(mesh):
    return jax.shard_map(
        body,
        mesh=mesh,
        in_specs=(
            P("panel", None, None, "obs"),
            P("obs"),
            P(None, "obs"),
            P(),
            P("obs", None, None, "panel"),
            P("obs", "panel"),
        ),
        out_specs=P("panel", "obs"),
        check_vma=False,
    )
```

time: 64.8 us -> 50.8 us (0.78)
  the two profiles are of different devices: /device:TPU:1 before, /device:TPU:2 now
where the time goes in v2:
time: 50.8 us; the launch traced here: 50.6 us
  Pallas kernels  48.7 us (96%)
  local copies, waits for them, and re-layouts  1.28 us (3%)
  between operations  0.66 us (1%)
    pallas_call x1, Pallas kernels, body(): pl.pallas_call(kernel, out_shape=jax.ShapeDtypeStruct((8, 128), F32), in_...  48.7 us
    unnamed x1, local copies, waits for them, and re-layouts  1.28 us

profile of v2, /device:TPU:2, one launch (start us, length us, event | category | flops | bytes accessed | tf_op | source)
XLA Modules:
  0.0 50.6 jit_solution(2712065729152871242)
XLA Ops:
  0.7 48.7 %shard_map.64 = f32[8,128]{1,0:T(8,128)} custom-call(bf16[4000,128]{1,0:T(8,128)(2,1)} %bitcast.4, s32[1,1024]{1,0:T(1,128)} %bitcast.7, f32[3,1024]{1,0:T(4,128)} %coord_ref.1, s32[64,128]{1,0:T(8,128)} %bitcast.6, bf16[2048,128]{1,0:T(8,128)(2,1)} %bitcast.5, s32[1,1]{1,0:T(1,128)S(6)} %copy.8.off_ref), custom_call_target="tpu_custom_call" | custom-call | tf_op jit(solution)/shard_map/pallas_call | solution.py:396
  49.3 1.3 %copy.9 = f32[8,128]{1,0:T(8,128)} copy(f32[8,128]{1,0:T(8,128)} %shard_map.64) | data formatting | bytes 8192

commit v3 on v2

--- a/solution.py
+++ b/solution.py
@@ -19,7 +19,10 @@
 MESH = pl.DeviceIdType.MESH
 GROUPS = ((0, 112), (112, 96), (208, 48))
 GROUP_ENDS = (7, 13, 16)
-OBS_ORDER = (4, 3, 5, 2, 6, 7, 1)
+AWAY = (0, 1, 15, 2, 14, 3, 13, 4, 12, 5, 11, 6, 10, 7, 9, 8)
+Z_FAR = AWAY[:0:-1]
+OBS_FAR = (5, 4, 3, 7, 2, 6, 1, 0)
+BACK = (0, 1, 6, 7, 4, 5, 2, 3)
 
 
 def iota(shape, axis):
@@ -42,8 +45,8 @@
     return jnp.where(low, a, pltpu.roll(b, 4, 0)), jnp.where(low, pltpu.roll(a, 4, 0), b)
 
 
-def fill_table(coord_ref, table):
-    def table_step(tile, carry):
+def fill_table(coord_ref, table, greet):
+    def table_step(tile):
         lanes = pl.ds(pl.multiple_of(tile * 128, 128), 128)
         factors = []
         for direction in range(3):
@@ -62,9 +65,17 @@
         nodes = [pairs[n // 25][(n // 5) % 5] * factors[2][n % 5] for n in range(125)]
         for j in range(125):
             table[8 * j:8 * j + 8, lanes] = jnp.where(low, nodes[(2 * j) % 125], nodes[(2 * j + 1) % 125])
+
+    def table_loop(tile, carry):
+        for k in range(4):
+            greet(4 * tile + k)
+        table_step(tile)
         return carry
 
-    lax.fori_loop(0, 8, table_step, 0)
+    lax.fori_loop(1, 8, table_loop, 0)
+    for k in range(1, 4):
+        greet(k)
+    table_step(0)
 
 
 def fill_sources(donor, hot, table, src):
@@ -163,14 +174,15 @@
         w2_ref[k * 128:k * 128 + 128, :] = dot(rows, mover, NN).astype(BF16)
 
 
-def fill_messages(base_in, ex_in, msg):
+def fill_messages(x, base_in, ex_in, msg):
     low = iota((8, 128), 0) < 4
     lane = iota((8, 128), 1)
     sums = []
     for px in range(NX):
-        total = ex_in[px * NB].astype(F32)
+        first = lax.rem(px + NX - x, NX) * NB
+        total = ex_in[first].astype(F32)
         for pb in range(1, NB):
-            total = total + ex_in[px * NB + pb].astype(F32)
+            total = total + ex_in[first + pb].astype(F32)
         sums.append(total)
     quants = []
     for v in range(2):
@@ -178,7 +190,7 @@
         e01, o01 = mix_pair(sums[0][rows], sums[1][rows], low)
         e23, o23 = mix_pair(sums[2][rows], sums[3][rows], low)
         quants += [(e01, e23), (o01, o23)]
-    bases = [base_in[px].astype(F32) for px in range(NX)]
+    bases = [base_in[lax.rem(px + NX - x, NX)].astype(F32) for px in range(NX)]
     masks = [((lane & 63) >= 16 * q + 12) & ((lane & 63) < 16 * q + 16) for q in range(4)]
     for v in range(8):
         rows = slice(v * 8, v * 8 + 8)
@@ -195,15 +207,19 @@
             msg[pz] = jnp.concatenate(done, axis=0).astype(BF16)
 
 
-def kernel(donor_hbm, elem_ref, coord_ref, owner_ref, w_hbm, off_ref, out_ref,
-           donor, weights, table, hot, src, wf, w2, base_out, ex_out,
-           base_in, ex_in, msg, held, wide, part, part_b, part_in, line, line_in,
+def kernel(donor_hbm, elem_hbm, coord_hbm, owner_hbm, w_hbm, off_ref, out_ref,
+           donor, elem_ref, coord_ref, owner_ref, weights, table, hot, src, wf, w2, base_out, ex_out,
+           base_in, ex_in, msg, held, wide, part_b, part_in, line, line_in,
            base_s, base_r, ex_s, ex_r, z_s, z_r, o_s, o_r, px_s, px_r, pz_s, pz_r, own_sem):
     panel = lax.axis_index("panel")
     b = lax.axis_index("obs")
-    x = panel // NZ
-    z = panel % NZ
-    me = x * NB + b
+    x = lax.div(panel, NZ)
+    z = lax.rem(panel, NZ)
+    y = lax.div(b, 2)
+    core = lax.rem(b, 2)
+    xs = [lax.rem(x + i, NX) for i in range(NX)]
+    zs = [lax.rem(z + i, NZ) for i in range(NZ)]
+    bs = [lax.rem(y + i // 2, 4) * 2 + (core if i % 2 == 0 else 1 - core) for i in range(NB)]
 
     def at(px, pz, pb):
         return {"panel": px * NZ + pz, "obs": pb}
@@ -213,104 +229,107 @@
             src_ref=src_ref, dst_ref=dst_ref, send_sem=send, recv_sem=recv,
             device_id=device, device_id_type=MESH)
 
-    donor_copy = pltpu.make_async_copy(donor_hbm, donor, own_sem.at[0])
-    weight_copy = pltpu.make_async_copy(w_hbm, weights, own_sem.at[1])
-    donor_copy.start()
-    weight_copy.start()
+    loads = [
+        pltpu.make_async_copy(source, target, own_sem.at[i])
+        for i, (source, target) in enumerate((
+            (coord_hbm, coord_ref), (elem_hbm, elem_ref), (owner_hbm, owner_ref), (donor_hbm, donor),
+            (w_hbm, weights)))
+    ]
+    for load in loads:
+        load.start()
     barrier = pltpu.get_barrier_semaphore()
 
-    def greet(i, c):
-        slot = (me + i) % 32
-        pl.semaphore_signal(barrier, inc=1, device_id=at(slot // NB, z, slot % NB), device_id_type=MESH)
-        return c
-
-    def greet_z(i, c):
-        pl.semaphore_signal(barrier, inc=1, device_id=at(x, (z + i) % NZ, b), device_id_type=MESH)
-        return c
-
-    lax.fori_loop(1, NZ, greet_z, 0)
-    lax.fori_loop(1, 32, greet, 0)
-
-    fill_table(coord_ref, table)
+    def greet(i):
+        slot = lax.rem(x * NB + b + i, NX * NB)
+        pl.semaphore_signal(barrier, inc=1, device_id=at(lax.div(slot, NB), z, lax.rem(slot, NB)),
+                            device_id_type=MESH)
+
+    for i in Z_FAR:
+        pl.semaphore_signal(barrier, inc=1, device_id=at(x, zs[i], b), device_id_type=MESH)
+    loads[0].wait()
+    fill_table(coord_ref, table, greet)
+    loads[1].wait()
+    loads[2].wait()
     hot[...] = hit(iota((128, 1024), 0) == elem_ref[...] - b * 128)
-    own = flat_row(owner_ref[pl.ds(b * 8, 8), :])
+    own = flat_row(owner_ref[pl.ds(pl.multiple_of(b * 8, 8), 8), :])
     rank = rank_points(own)
-    donor_copy.wait()
+    loads[3].wait()
     fill_sources(donor, hot, table, src)
     sources = jnp.concatenate([src[tile] for tile in range(8)], axis=1).astype(BF16).astype(F32)
     group_extra(sources, own, rank, ex_out)
+    pl.semaphore_wait(barrier, 46)
+
+    def ex_copy(i, j):
+        px, pb = xs[i], bs[j]
+        back = ((NX - i) % NX) * NB + BACK[j]
+        return remote(ex_out.at[pl.ds(pl.multiple_of((px * NB + pb) * 16, 16), 16)], ex_in.at[back],
+                      ex_s.at[back], ex_r.at[back], at(px, z, pb))
+
+    def base_copy(i):
+        back = (NX - i) % NX
+        return remote(base_out.at[pl.ds(pl.multiple_of(xs[i] * 64, 64), 64)], base_in.at[back],
+                      base_s.at[back], base_r.at[back], at(xs[i], z, b))
+
+    around = [(i, j) for i in (2, 1, 3, 0) for j in OBS_FAR if i or j]
+    for i, j in around:
+        ex_copy(i, j).start()
     group_base(sources, own, rank, base_out)
-    pl.semaphore_wait(barrier, 46)
-
-    def base_copy(px, source):
-        return remote(base_out.at[pl.ds(px * 64, 64)], base_in.at[source], base_s.at[px], base_r.at[source],
-                      at(px, z, b))
-
-    def ex_copy(slot, source):
-        return remote(ex_out.at[pl.ds(slot * 16, 16)], ex_in.at[source], ex_s.at[slot], ex_r.at[source],
-                      at(slot // NB, z, slot % NB))
-
-    def ex_start(j, c):
-        ex_copy((me + 12 + j + j // 20) % 32, me).start()
-        return c
-
     for i in (2, 1, 3):
-        base_copy((x + i) % NX, x).start()
-    lax.fori_loop(0, 31, ex_start, 0)
-    weight_copy.wait()
-    own_base = pltpu.make_async_copy(base_out.at[pl.ds(x * 64, 64)], base_in.at[x], own_sem.at[0])
-    own_ex = pltpu.make_async_copy(ex_out.at[pl.ds(me * 16, 16)], ex_in.at[me], own_sem.at[1])
+        base_copy(i).start()
+    own_base = pltpu.make_async_copy(base_out.at[pl.ds(pl.multiple_of(x * 64, 64), 64)], base_in.at[0], own_sem.at[0])
+    own_ex = pltpu.make_async_copy(ex_out.at[pl.ds(pl.multiple_of((x * NB + b) * 16, 16), 16)], ex_in.at[0],
+                                   own_sem.at[1])
     own_base.start()
     own_ex.start()
+    loads[4].wait()
     wide[:, 0:FRONT, :] = jnp.zeros((4, FRONT, 128), F32)
     order_weights(weights, owner_ref, panel, wf, w2)
     own_base.wait()
     own_ex.wait()
-
-    def ex_wait(i, c):
-        ex_copy((me + i) % 32, (me + i) % 32).wait_recv()
-        return c
-
+    for i, j in around[::-1]:
+        ex_copy(i, j).wait_recv()
     for i in (1, 3, 2):
-        base_copy((x + i) % NX, (x + i) % NX).wait_recv()
-    lax.fori_loop(1, 32, ex_wait, 0)
-    fill_messages(base_in, ex_in, msg)
-
-    def away(i):
-        h = (i + 1) // 2
-        return h + (1 - i % 2) * (NZ - 2 * h)
+        base_copy(i).wait_recv()
+    fill_messages(x, base_in, ex_in, msg)
 
     def z_copy(i):
-        pz = (z + NZ - away(i)) % NZ
+        pz = zs[NZ - AWAY[i]]
         return remote(msg.at[pz], held.at[b, pl.ds(i * 16, 16)], z_s.at[i], z_r.at[i], at(x, pz, b))
 
-    def z_start(i, c):
-        z_copy(NZ - i).start()
-        return c
-
-    def z_wait(i, c):
-        z_copy(i).wait_recv()
-        return c
-
-    lax.fori_loop(1, NZ, z_start, 0)
+    for i in range(NZ - 1, 0, -1):
+        z_copy(i).start()
     own_z = pltpu.make_async_copy(msg.at[z], held.at[b, pl.ds(0, 16)], own_sem.at[0])
     own_z.start()
     own_z.wait()
 
-    def o_copy(g, pb, source):
+    def o_copy(g, source, j, place):
         rows = pl.ds(*GROUPS[g])
-        return remote(held.at[source, rows], held.at[source, rows], o_s.at[g * NB + pb], o_r.at[g * NB + source],
-                      at(x, z, pb))
+        return remote(held.at[source, rows], held.at[source, rows], o_s.at[g * NB + place], o_r.at[g * NB + place],
+                      at(x, z, bs[j]))
+
+    def own_out(g, j):
+        return o_copy(g, b, j, BACK[j])
+
+    def pass_on(g, j):
+        return o_copy(g, bs[j], 1, j + 1)
 
     begin = 1
     for g in range(3):
-        lax.fori_loop(begin, GROUP_ENDS[g], z_wait, 0)
+        for i in range(begin, GROUP_ENDS[g]):
+            z_copy(i).wait_recv()
         begin = GROUP_ENDS[g]
-        for i in OBS_ORDER:
-            o_copy(g, (b + i) % NB, b).start()
-    for g in range(3):
-        for i in range(1, NB):
-            o_copy(g, (b + i) % NB, (b + i) % NB).wait_recv()
+        for j in ((4, 2, 6, 1) if g < 2 else (5, 4, 3, 7, 2, 6, 1)):
+            own_out(g, j).start()
+    for g in range(2):
+        for j in (2, 6, 4):
+            own_out(g, BACK[j]).wait_recv()
+            pass_on(g, j).start()
+    for j in range(1, NB):
+        own_out(2, BACK[j]).wait_recv()
+    for g in range(2):
+        own_out(g, 1).wait_recv()
+        for j in (2, 6, 4):
+            pass_on(g, j).wait_recv()
 
     low_wide = iota((8, 512), 0) < 4
     halves = []
@@ -319,7 +338,7 @@
         left = jnp.concatenate([held[pb][:, cols] for pb in range(NB)], axis=1)
         halves.append(dot(left, w2[...], NT))
     for i in range(NZ):
-        time = FRONT + 8 * ((z + away(i)) % NZ)
+        time = FRONT + 8 * zs[AWAY[i]]
         for xp in range(2):
             rows = slice(i * 16 + xp * 8, i * 16 + xp * 8 + 8)
             pair = mix_pair(halves[0][rows], halves[1][rows], low_wide)
@@ -328,78 +347,72 @@
                 for k in range(4):
                     wide[k, pl.ds(start, 8), :] = pair[side][:, k * 128:k * 128 + 128]
     delay = off_ref[0, 0]
-    total = wide[0, pl.ds(FRONT - delay, TW), :]
-    for k in range(1, 4):
-        total = total + wide[k, pl.ds(FRONT - delay - k, TW), :]
-    part[...] = total
-    part_b[...] = total.astype(BF16).reshape(NX, 128, 128)
+
+    def block(px):
+        start = FRONT - delay + px * 128
+        total = wide[0, pl.ds(start, 128), :]
+        for k in range(1, 4):
+            total = total + wide[k, pl.ds(start - k, 128), :]
+        return total
 
     def px_copy(i):
-        px = (x + NX - i) % NX
-        return remote(part_b.at[px], part_in.at[i], px_s.at[i], px_r.at[i], at(px, z, b))
+        px = xs[NX - i]
+        return remote(part_b.at[i], part_in.at[i], px_s.at[i], px_r.at[i], at(px, z, b))
 
     for i in (2, 1, 3):
+        part_b[i] = block(xs[NX - i]).astype(BF16)
         px_copy(i).start()
-    acc = part[pl.ds(pl.multiple_of(x * 128, 128), 128), :]
+    acc = block(x)
     for i in (1, 3, 2):
         px_copy(i).wait_recv()
         acc = acc + part_in[i].astype(F32)
     line[...] = acc
 
     def pz_copy(i):
-        pz = (z + NZ - away(i)) % NZ
-        return remote(line.at[pl.ds(pz * 8, 8)], line_in.at[i], pz_s.at[i], pz_r.at[i], at(x, pz, b))
-
-    def pz_start(i, c):
-        pz_copy(NZ - i).start()
-        return c
-
-    def pz_wait(i, c):
+        pz = zs[NZ - AWAY[i]]
+        return remote(line.at[pl.ds(pl.multiple_of(pz * 8, 8), 8)], line_in.at[i], pz_s.at[i], pz_r.at[i],
+                      at(x, pz, b))
+
+    for i in range(NZ - 1, 0, -1):
+        pz_copy(i).start()
+
+    for i, j in around:
+        ex_copy(i, j).wait_send()
+    for i in range(1, NX):
+        base_copy(i).wait_send()
+        px_copy(i).wait_send()
+    for i in range(1, NZ):
+        z_copy(i).wait_send()
+    for g in range(2):
+        for j in (4, 2, 6, 1):
+            own_out(g, j).wait_send()
+        for j in (2, 6, 4):
+            pass_on(g, j).wait_send()
+    for j in range(1, NB):
+        own_out(2, j).wait_send()
+    for i in range(1, NZ):
+        pz_copy(i).wait_send()
+
+    acc = line[pl.ds(pl.multiple_of(z * 8, 8), 8), :]
+    for i in range(1, NZ):
         pz_copy(i).wait_recv()
-        return c
-
-    lax.fori_loop(1, NZ, pz_start, 0)
-
-    def ex_end(i, c):
-        ex_copy((me + i) % 32, me).wait_send()
-        return c
-
-    def z_end(i, c):
-        z_copy(i).wait_send()
-        return c
-
-    def pz_end(i, c):
-        pz_copy(i).wait_send()
-        return c
-
-    for i in range(1, NX):
-        base_copy((x + i) % NX, x).wait_send()
-        px_copy(i).wait_send()
-    lax.fori_loop(1, 32, ex_end, 0)
-    lax.fori_loop(1, NZ, z_end, 0)
-    for g in range(3):
-        for i in range(1, NB):
-            o_copy(g, (b + i) % NB, b).wait_send()
-    lax.fori_loop(1, NZ, pz_end, 0)
-
-    acc = line[pl.ds(pl.multiple_of(z * 8, 8), 8), :]
-    lax.fori_loop(1, NZ, pz_wait, 0)
-    for i in range(1, NZ):
         acc = acc + line_in[i]
     out_ref[...] = acc
 
 
 def body(donor, donor_elem, local_coords, owner, weights, offsets):
-    vmem = pl.BlockSpec(memory_space=pltpu.VMEM)
-    anywhere = pl.BlockSpec(memory_space=pl.ANY)
+    hbm = pl.BlockSpec(memory_space=pltpu.HBM)
     dma = pltpu.SemaphoreType.DMA
     return pl.pallas_call(
         kernel,
         out_shape=jax.ShapeDtypeStruct((8, 128), F32),
-        in_specs=[anywhere, vmem, vmem, vmem, anywhere, pl.BlockSpec(memory_space=pltpu.SMEM)],
-        out_specs=vmem,
+        in_specs=[hbm] * 5 + [pl.BlockSpec(memory_space=pltpu.SMEM)],
+        out_specs=pl.BlockSpec(memory_space=pltpu.VMEM),
         scratch_shapes=[
             pltpu.VMEM((4000, 128), BF16),
+            pltpu.VMEM((1, 1024), I32),
+            pltpu.VMEM((3, 1024), F32),
+            pltpu.VMEM((64, 128), I32),
             pltpu.VMEM((2048, 128), BF16),
             pltpu.VMEM((1000, 1024), F32),
             pltpu.VMEM((128, 1024), BF16),
@@ -413,13 +426,12 @@
             pltpu.VMEM((NZ, 16, 128), BF16),
             pltpu.VMEM((NB, 256, 128), BF16),
             pltpu.VMEM((4, FRONT + TW, 128), F32),
-            pltpu.VMEM((TW, 128), F32),
             pltpu.VMEM((NX, 128, 128), BF16),
             pltpu.VMEM((NX, 128, 128), BF16),
             pltpu.VMEM((128, 128), F32),
             pltpu.VMEM((NZ, 8, 128), F32),
             dma((NX,)), dma((NX,)), dma((32,)), dma((32,)), dma((NZ,)), dma((NZ,)),
-            dma((3 * NB,)), dma((3 * NB,)), dma((NX,)), dma((NX,)), dma((NZ,)), dma((NZ,)), dma((2,)),
+            dma((3 * NB,)), dma((3 * NB,)), dma((NX,)), dma((NX,)), dma((NZ,)), dma((NZ,)), dma((5,)),
         ],
         compiler_params=pltpu.CompilerParams(
             collective_id=0, has_side_effects=True, vmem_limit_bytes=60 * 2**20),

time: 50.8 us -> 48.7 us (0.959)
  the two profiles are of different devices: /device:TPU:2 before, /device:TPU:1 now
where the time goes in v3:
time: 48.7 us; the launch traced here: 48.5 us
  Pallas kernels  46.6 us (96%)
  local copies, waits for them, and re-layouts  1.28 us (3%)
  between operations  0.66 us (1%)
    pallas_call x1, Pallas kernels, body(): pl.pallas_call(kernel, out_shape=jax.ShapeDtypeStruct((8, 128), F32), in_...  46.6 us
    unnamed x1, local copies, waits for them, and re-layouts  1.28 us

profile of v3, /device:TPU:1, one launch (start us, length us, event | category | flops | bytes accessed | tf_op | source)
XLA Modules:
  0.0 48.5 jit_solution(17208634398509088902)
XLA Ops:
  0.7 46.6 %shard_map.64 = f32[8,128]{1,0:T(8,128)} custom-call(bf16[4000,128]{1,0:T(8,128)(2,1)} %bitcast.4, s32[1,1024]{1,0:T(1,128)} %bitcast.7, f32[3,1024]{1,0:T(4,128)} %coord_hbm.1, s32[64,128]{1,0:T(8,128)} %bitcast.6, bf16[2048,128]{1,0:T(8,128)(2,1)} %bitcast.5, s32[1,1]{1,0:T(1,128)S(6)} %copy.8.off_ref), custom_call_target="tpu_custom_call" | custom-call | tf_op jit(solution)/shard_map/pallas_call | solution.py:406
  47.2 1.3 %copy.9 = f32[8,128]{1,0:T(8,128)} copy(f32[8,128]{1,0:T(8,128)} %shard_map.64) | data formatting | bytes 8192

commit v4 on v3

--- a/solution.py
+++ b/solution.py
@@ -78,27 +78,31 @@
     table_step(0)
 
 
-def fill_sources(donor, hot, table, src):
-    def point_step(tile, carry):
-        lanes = pl.ds(pl.multiple_of(tile * 256, 256), 256)
-        for part in range(2):
-            picked = dot(donor[part * 2000:part * 2000 + 2000, :], hot[:, lanes], NN)
-            for half in range(2):
-                prod = picked[half * 1000:half * 1000 + 1000] * table[:, lanes]
-                prod = prod.reshape(125, 8, 256)
-                first = jnp.sum(prod[:62], axis=0)
-                last = jnp.sum(prod[63:], axis=0)
-                mid = prod[62]
-                step = 16 * part + 2 * half
-                even = first[:4] + first[4:] + mid[:4]
-                odd = last[:4] + last[4:] + mid[4:]
-                for side in range(2):
-                    cols = slice(side * 128, side * 128 + 128)
-                    src[2 * tile + side, pl.ds(step, 4, stride=4), :] = even[:, cols]
-                    src[2 * tile + side, pl.ds(step + 1, 4, stride=4), :] = odd[:, cols]
-        return carry
-
-    lax.fori_loop(0, 4, point_step, 0)
+def fill_sources(donor, hot, table, src, ready):
+    edges = (0, 62, 63, 125, 187, 188, 250)
+    for part in range(2):
+        ready(part)
+        sums = [None] * 6
+        for piece in range(5):
+            row = part * 2000 + piece * 400
+            picked = dot(donor[row:row + 400, :], hot[...], NN)
+            for k in range(6):
+                begin, end = max(edges[k], piece * 50), min(edges[k + 1], piece * 50 + 50)
+                if begin < end:
+                    at = 8 * (begin - piece * 50)
+                    size = 8 * (end - begin)
+                    prod = picked[at:at + size] * table[8 * (begin % 125):8 * (begin % 125) + size, :]
+                    value = jnp.sum(prod.reshape(end - begin, 8, 1024), axis=0)
+                    sums[k] = value if sums[k] is None else sums[k] + value
+        for half in range(2):
+            first, mid, last = sums[3 * half:3 * half + 3]
+            step = 16 * part + 2 * half
+            even = first[:4] + first[4:] + mid[:4]
+            odd = last[:4] + last[4:] + mid[4:]
+            for tile in range(8):
+                cols = slice(tile * 128, tile * 128 + 128)
+                src[tile, pl.ds(step, 4, stride=4), :] = even[:, cols]
+                src[tile, pl.ds(step + 1, 4, stride=4), :] = odd[:, cols]
 
 
 def rank_points(own):
@@ -117,12 +121,17 @@
     return jnp.concatenate(ranks, axis=1).astype(I32)
 
 
-def group_base(sources, own, rank, base_ref):
+def fill_places(own, rank, place_base, place_extra):
     spot = jnp.where(rank < 12, (own & 7) * 16 + rank, -1)
-    place = hit(iota((128, 1024), 0) == spot)
+    place_base[...] = hit(iota((128, 1024), 0) == spot)
+    spot = jnp.where(rank >= 12, ((own >> 4) & 1) * 64 + (own & 15) * 4 + (rank & 3), -1)
+    place_extra[...] = hit(iota((128, 1024), 0) == spot)
+
+
+def group_base(sources, own, place, base_ref):
     group = own >> 3
     left = jnp.concatenate([jnp.where(group == g, sources, 0.0).astype(BF16) for g in range(8)], axis=0)
-    grouped = dot(left, place, NT)
+    grouped = dot(left, place[...], NT)
     row = iota((32, 128), 0)
     lane = iota((32, 128), 1)
     for g in range(8):
@@ -136,16 +145,13 @@
         base_ref[g * 32:g * 32 + 32, :] = x.astype(BF16)
 
 
-def group_extra(sources, own, rank, ex_ref):
-    extra = rank - 12
-    spot = jnp.where(rank >= 12, ((own >> 4) & 1) * 64 + (own & 15) * 4 + (extra & 3), -1)
-    place = hit(iota((128, 1024), 0) == spot)
-    group = (own >> 5) * 8 + (extra >> 2)
+def group_extra(sources, own, rank, place, ex_ref):
+    group = (own >> 5) * 8 + ((rank - 12) >> 2)
     half = iota((16, 128), 1) < 64
     for g in range(2):
         left = jnp.concatenate(
             [jnp.where(group == g * 8 + h, sources, 0.0).astype(BF16) for h in range(8)], axis=0)
-        more = dot(left, place, NT)
+        more = dot(left, place[...], NT)
         for h in range(8):
             r0, r1 = more[h * 32:h * 32 + 16], more[h * 32 + 16:h * 32 + 32]
             even = jnp.where(half, r0, pltpu.roll(r1, 64, 1))
@@ -208,7 +214,7 @@
 
 
 def kernel(donor_hbm, elem_hbm, coord_hbm, owner_hbm, w_hbm, off_ref, out_ref,
-           donor, elem_ref, coord_ref, owner_ref, weights, table, hot, src, wf, w2, base_out, ex_out,
+           donor, elem_ref, coord_ref, owner_ref, weights, place_base, place_extra, table, hot, src, wf, w2, base_out, ex_out,
            base_in, ex_in, msg, held, wide, part_b, part_in, line, line_in,
            base_s, base_r, ex_s, ex_r, z_s, z_r, o_s, o_r, px_s, px_r, pz_s, pz_r, own_sem):
     panel = lax.axis_index("panel")
@@ -232,7 +238,8 @@
     loads = [
         pltpu.make_async_copy(source, target, own_sem.at[i])
         for i, (source, target) in enumerate((
-            (coord_hbm, coord_ref), (elem_hbm, elem_ref), (owner_hbm, owner_ref), (donor_hbm, donor),
+            (coord_hbm, coord_ref), (elem_hbm, elem_ref), (owner_hbm, owner_ref),
+            (donor_hbm.at[0:2000], donor.at[0:2000]), (donor_hbm.at[2000:4000], donor.at[2000:4000]),
             (w_hbm, weights)))
     ]
     for load in loads:
@@ -253,10 +260,10 @@
     hot[...] = hit(iota((128, 1024), 0) == elem_ref[...] - b * 128)
     own = flat_row(owner_ref[pl.ds(pl.multiple_of(b * 8, 8), 8), :])
     rank = rank_points(own)
-    loads[3].wait()
-    fill_sources(donor, hot, table, src)
+    fill_places(own, rank, place_base, place_extra)
+    fill_sources(donor, hot, table, src, lambda part: loads[3 + part].wait())
     sources = jnp.concatenate([src[tile] for tile in range(8)], axis=1).astype(BF16).astype(F32)
-    group_extra(sources, own, rank, ex_out)
+    group_extra(sources, own, rank, place_extra, ex_out)
     pl.semaphore_wait(barrier, 46)
 
     def ex_copy(i, j):
@@ -273,7 +280,7 @@
     around = [(i, j) for i in (2, 1, 3, 0) for j in OBS_FAR if i or j]
     for i, j in around:
         ex_copy(i, j).start()
-    group_base(sources, own, rank, base_out)
+    group_base(sources, own, place_base, base_out)
     for i in (2, 1, 3):
         base_copy(i).start()
     own_base = pltpu.make_async_copy(base_out.at[pl.ds(pl.multiple_of(x * 64, 64), 64)], base_in.at[0], own_sem.at[0])
@@ -281,7 +288,7 @@
                                    own_sem.at[1])
     own_base.start()
     own_ex.start()
-    loads[4].wait()
+    loads[5].wait()
     wide[:, 0:FRONT, :] = jnp.zeros((4, FRONT, 128), F32)
     order_weights(weights, owner_ref, panel, wf, w2)
     own_base.wait()
@@ -414,6 +421,8 @@
             pltpu.VMEM((3, 1024), F32),
             pltpu.VMEM((64, 128), I32),
             pltpu.VMEM((2048, 128), BF16),
+            pltpu.VMEM((128, 1024), BF16),
+            pltpu.VMEM((128, 1024), BF16),
             pltpu.VMEM((1000, 1024), F32),
             pltpu.VMEM((128, 1024), BF16),
             pltpu.VMEM((8, 32, 128), F32),
@@ -431,10 +440,10 @@
             pltpu.VMEM((128, 128), F32),
             pltpu.VMEM((NZ, 8, 128), F32),
             dma((NX,)), dma((NX,)), dma((32,)), dma((32,)), dma((NZ,)), dma((NZ,)),
-            dma((3 * NB,)), dma((3 * NB,)), dma((NX,)), dma((NX,)), dma((NZ,)), dma((NZ,)), dma((5,)),
+            dma((3 * NB,)), dma((3 * NB,)), dma((NX,)), dma((NX,)), dma((NZ,)), dma((NZ,)), dma((6,)),
         ],
         compiler_params=pltpu.CompilerParams(
-            collective_id=0, has_side_effects=True, vmem_limit_bytes=60 * 2**20),
+            collective_id=0, has_side_effects=True, vmem_limit_bytes=55228 * 1024),
     )(
         donor.reshape(4000, 128),
         donor_elem.reshape(1, 1024),

time: 48.7 us -> 47.5 us (0.975)
  local copies, waits for them, and re-layouts: 1.28 us -> 0.6 us
  Pallas kernels: 46.6 us -> 46 us
    unnamed x1, local copies, waits for them, and re-layouts: 1.28 us -> 0.6 us
    pallas_call x1, Pallas kernels: 46.6 us -> 46 us  [body(): pl.pallas_call(kernel, out_shape=jax.ShapeDtypeStruct((8, 128), F32), in_...]
where the time goes in v4:
time: 47.5 us; the launch traced here: 47.3 us
  Pallas kernels  46 us (97%)
  between operations  0.66 us (1%)
  local copies, waits for them, and re-layouts  0.6 us (1%)
    pallas_call x1, Pallas kernels, body(): pl.pallas_call(kernel, out_shape=jax.ShapeDtypeStruct((8, 128), F32), in_...  46 us

profile of v4, /device:TPU:1, one launch (start us, length us, event | category | flops | bytes accessed | tf_op | source)
XLA Modules:
  0.0 47.3 jit_solution(14038636426256588421)
XLA Ops:
  0.7 46.0 %shard_map.64 = f32[8,128]{1,0:T(8,128)S(1)} custom-call(bf16[4000,128]{1,0:T(8,128)(2,1)} %bitcast.4, s32[1,1024]{1,0:T(1,128)} %bitcast.7, f32[3,1024]{1,0:T(4,128)} %coord_hbm.1, s32[64,128]{1,0:T(8,128)} %bitcast.6, bf16[2048,128]{1,0:T(8,128)(2,1)} %bitcast.5, s32[1,1]{1,0:T(1,128)S(6)} %copy.8.off_ref), custom_call_target="tpu_custom_call" | custom-call | tf_op jit(solution)/shard_map/pallas_call | solution.py:413
  46.7 0.6 %copy.9 = f32[8,128]{1,0:T(8,128)} copy(f32[8,128]{1,0:T(8,128)S(1)} %shard_map.64) | data formatting | bytes 8192

commit v5 on v4

--- a/solution.py
+++ b/solution.py
@@ -23,6 +23,8 @@
 Z_FAR = AWAY[:0:-1]
 OBS_FAR = (5, 4, 3, 7, 2, 6, 1, 0)
 BACK = (0, 1, 6, 7, 4, 5, 2, 3)
+BASE_S, BASE_R, EX_S, EX_R, Z_S, Z_R, Y_R, O_S, O_R, PX_S, PX_R, PZ_S, PZ_R, OWN = (
+    0, 1, 2, 3, 4, 5, 8, 10, 13, 16, 17, 18, 19, 20)
 
 
 def iota(shape, axis):
@@ -216,7 +218,7 @@
 def kernel(donor_hbm, elem_hbm, coord_hbm, owner_hbm, w_hbm, off_ref, out_ref,
            donor, elem_ref, coord_ref, owner_ref, weights, place_base, place_extra, table, hot, src, wf, w2, base_out, ex_out,
            base_in, ex_in, msg, held, wide, part_b, part_in, line, line_in,
-           base_s, base_r, ex_s, ex_r, z_s, z_r, o_s, o_r, px_s, px_r, pz_s, pz_r, own_sem):
+           sems):
     panel = lax.axis_index("panel")
     b = lax.axis_index("obs")
     x = lax.div(panel, NZ)
@@ -232,11 +234,14 @@
 
     def remote(src_ref, dst_ref, send, recv, device):
         return pltpu.make_async_remote_copy(
-            src_ref=src_ref, dst_ref=dst_ref, send_sem=send, recv_sem=recv,
+            src_ref=src_ref, dst_ref=dst_ref, send_sem=sems.at[send], recv_sem=sems.at[recv],
             device_id=device, device_id_type=MESH)
 
+    def settle(ref, which):
+        pltpu.make_async_copy(ref, ref, sems.at[which]).wait()
+
     loads = [
-        pltpu.make_async_copy(source, target, own_sem.at[i])
+        pltpu.make_async_copy(source, target, sems.at[OWN + i])
         for i, (source, target) in enumerate((
             (coord_hbm, coord_ref), (elem_hbm, elem_ref), (owner_hbm, owner_ref),
             (donor_hbm.at[0:2000], donor.at[0:2000]), (donor_hbm.at[2000:4000], donor.at[2000:4000]),
@@ -270,12 +275,12 @@
         px, pb = xs[i], bs[j]
         back = ((NX - i) % NX) * NB + BACK[j]
         return remote(ex_out.at[pl.ds(pl.multiple_of((px * NB + pb) * 16, 16), 16)], ex_in.at[back],
-                      ex_s.at[back], ex_r.at[back], at(px, z, pb))
+                      EX_S, EX_R, at(px, z, pb))
 
     def base_copy(i):
         back = (NX - i) % NX
         return remote(base_out.at[pl.ds(pl.multiple_of(xs[i] * 64, 64), 64)], base_in.at[back],
-                      base_s.at[back], base_r.at[back], at(xs[i], z, b))
+                      BASE_S, BASE_R, at(xs[i], z, b))
 
     around = [(i, j) for i in (2, 1, 3, 0) for j in OBS_FAR if i or j]
     for i, j in around:
@@ -283,9 +288,9 @@
     group_base(sources, own, place_base, base_out)
     for i in (2, 1, 3):
         base_copy(i).start()
-    own_base = pltpu.make_async_copy(base_out.at[pl.ds(pl.multiple_of(x * 64, 64), 64)], base_in.at[0], own_sem.at[0])
+    own_base = pltpu.make_async_copy(base_out.at[pl.ds(pl.multiple_of(x * 64, 64), 64)], base_in.at[0], sems.at[OWN])
     own_ex = pltpu.make_async_copy(ex_out.at[pl.ds(pl.multiple_of((x * NB + b) * 16, 16), 16)], ex_in.at[0],
-                                   own_sem.at[1])
+                                   sems.at[OWN + 1])
     own_base.start()
     own_ex.start()
     loads[5].wait()
@@ -293,50 +298,40 @@
     order_weights(weights, owner_ref, panel, wf, w2)
     own_base.wait()
     own_ex.wait()
-    for i, j in around[::-1]:
-        ex_copy(i, j).wait_recv()
-    for i in (1, 3, 2):
-        base_copy(i).wait_recv()
+    settle(ex_in.at[1:NX * NB], EX_R)
+    settle(base_in.at[1:NX], BASE_R)
     fill_messages(x, base_in, ex_in, msg)
 
     def z_copy(i):
         pz = zs[NZ - AWAY[i]]
-        return remote(msg.at[pz], held.at[b, pl.ds(i * 16, 16)], z_s.at[i], z_r.at[i], at(x, pz, b))
+        group = sum(i >= end for end in GROUP_ENDS)
+        return remote(msg.at[pz], held.at[b, pl.ds(i * 16, 16)], Z_S, Z_R + group, at(x, pz, b))
 
     for i in range(NZ - 1, 0, -1):
         z_copy(i).start()
-    own_z = pltpu.make_async_copy(msg.at[z], held.at[b, pl.ds(0, 16)], own_sem.at[0])
+    own_z = pltpu.make_async_copy(msg.at[z], held.at[b, pl.ds(0, 16)], sems.at[OWN])
     own_z.start()
     own_z.wait()
 
-    def o_copy(g, source, j, place):
+    def o_copy(g, source, j, recv):
         rows = pl.ds(*GROUPS[g])
-        return remote(held.at[source, rows], held.at[source, rows], o_s.at[g * NB + place], o_r.at[g * NB + place],
-                      at(x, z, bs[j]))
-
-    def own_out(g, j):
-        return o_copy(g, b, j, BACK[j])
-
-    def pass_on(g, j):
-        return o_copy(g, bs[j], 1, j + 1)
-
-    begin = 1
+        return remote(held.at[source, rows], held.at[source, rows], O_S + g, recv, at(x, z, bs[j]))
+
+    def pieces(g, n):
+        return held.at[0:n, pl.ds(*GROUPS[g])]
+
     for g in range(3):
-        for i in range(begin, GROUP_ENDS[g]):
-            z_copy(i).wait_recv()
-        begin = GROUP_ENDS[g]
+        first, size = GROUPS[g]
+        skip = 16 if g == 0 else 0
+        settle(held.at[b, pl.ds(first + skip, size - skip)], Z_R + g)
         for j in ((4, 2, 6, 1) if g < 2 else (5, 4, 3, 7, 2, 6, 1)):
-            own_out(g, j).start()
+            o_copy(g, b, j, Y_R + g if g < 2 and j > 1 else O_R + g).start()
     for g in range(2):
+        settle(pieces(g, 3), Y_R + g)
         for j in (2, 6, 4):
-            own_out(g, BACK[j]).wait_recv()
-            pass_on(g, j).start()
-    for j in range(1, NB):
-        own_out(2, BACK[j]).wait_recv()
-    for g in range(2):
-        own_out(g, 1).wait_recv()
-        for j in (2, 6, 4):
-            pass_on(g, j).wait_recv()
+            o_copy(g, bs[j], 1, O_R + g).start()
+    for g in range(3):
+        settle(pieces(g, 4 if g < 2 else 7), O_R + g)
 
     low_wide = iota((8, 512), 0) < 4
     halves = []
@@ -364,45 +359,36 @@
 
     def px_copy(i):
         px = xs[NX - i]
-        return remote(part_b.at[i], part_in.at[i], px_s.at[i], px_r.at[i], at(px, z, b))
+        return remote(part_b.at[i], part_in.at[i], PX_S, PX_R, at(px, z, b))
 
     for i in (2, 1, 3):
         part_b[i] = block(xs[NX - i]).astype(BF16)
         px_copy(i).start()
     acc = block(x)
+    settle(part_in.at[1:NX], PX_R)
     for i in (1, 3, 2):
-        px_copy(i).wait_recv()
         acc = acc + part_in[i].astype(F32)
     line[...] = acc
 
     def pz_copy(i):
         pz = zs[NZ - AWAY[i]]
-        return remote(line.at[pl.ds(pl.multiple_of(pz * 8, 8), 8)], line_in.at[i], pz_s.at[i], pz_r.at[i],
+        return remote(line.at[pl.ds(pl.multiple_of(pz * 8, 8), 8)], line_in.at[i], PZ_S, PZ_R,
                       at(x, pz, b))
 
     for i in range(NZ - 1, 0, -1):
         pz_copy(i).start()
 
-    for i, j in around:
-        ex_copy(i, j).wait_send()
-    for i in range(1, NX):
-        base_copy(i).wait_send()
-        px_copy(i).wait_send()
+    settle(ex_in.at[1:NX * NB], EX_S)
+    settle(base_in.at[1:NX], BASE_S)
+    settle(msg.at[1:NZ], Z_S)
+    for g in range(3):
+        settle(pieces(g, 7), O_S + g)
+    settle(part_in.at[1:NX], PX_S)
+    settle(line_in.at[1:NZ], PZ_S)
+
+    acc = line[pl.ds(pl.multiple_of(z * 8, 8), 8), :]
+    settle(line_in.at[1:NZ], PZ_R)
     for i in range(1, NZ):
-        z_copy(i).wait_send()
-    for g in range(2):
-        for j in (4, 2, 6, 1):
-            own_out(g, j).wait_send()
-        for j in (2, 6, 4):
-            pass_on(g, j).wait_send()
-    for j in range(1, NB):
-        own_out(2, j).wait_send()
-    for i in range(1, NZ):
-        pz_copy(i).wait_send()
-
-    acc = line[pl.ds(pl.multiple_of(z * 8, 8), 8), :]
-    for i in range(1, NZ):
-        pz_copy(i).wait_recv()
         acc = acc + line_in[i]
     out_ref[...] = acc
 
@@ -439,8 +425,7 @@
             pltpu.VMEM((NX, 128, 128), BF16),
             pltpu.VMEM((128, 128), F32),
             pltpu.VMEM((NZ, 8, 128), F32),
-            dma((NX,)), dma((NX,)), dma((32,)), dma((32,)), dma((NZ,)), dma((NZ,)),
-            dma((3 * NB,)), dma((3 * NB,)), dma((NX,)), dma((NX,)), dma((NZ,)), dma((NZ,)), dma((6,)),
+            dma((OWN + 6,)),
         ],
         compiler_params=pltpu.CompilerParams(
             collective_id=0, has_side_effects=True, vmem_limit_bytes=55228 * 1024),

time: 47.5 us -> 46.1 us (0.971)
  Pallas kernels: 46 us -> 44.6 us
    pallas_call x1, Pallas kernels: 46 us -> 44.6 us  [body(): pl.pallas_call(kernel, out_shape=jax.ShapeDtypeStruct((8, 128), F32), in_...]
where the time goes in v5:
time: 46.1 us; the launch traced here: 45.9 us
  Pallas kernels  44.6 us (97%)
  between operations  0.66 us (1%)
  local copies, waits for them, and re-layouts  0.6 us (1%)
    pallas_call x1, Pallas kernels, body(): pl.pallas_call(kernel, out_shape=jax.ShapeDtypeStruct((8, 128), F32), in_...  44.6 us

profile of v5, /device:TPU:1, one launch (start us, length us, event | category | flops | bytes accessed | tf_op | source)
XLA Modules:
  0.0 45.9 jit_solution(4596156834893256250)
XLA Ops:
  0.7 44.6 %shard_map.64 = f32[8,128]{1,0:T(8,128)S(1)} custom-call(bf16[4000,128]{1,0:T(8,128)(2,1)} %bitcast.4, s32[1,1024]{1,0:T(1,128)} %bitcast.7, f32[3,1024]{1,0:T(4,128)} %coord_hbm.1, s32[64,128]{1,0:T(8,128)} %bitcast.6, bf16[2048,128]{1,0:T(8,128)(2,1)} %bitcast.5, s32[1,1]{1,0:T(1,128)S(6)} %copy.8.off_ref), custom_call_target="tpu_custom_call" | custom-call | tf_op jit(solution)/shard_map/pallas_call | solution.py:399
  45.3 0.6 %copy.9 = f32[8,128]{1,0:T(8,128)} copy(f32[8,128]{1,0:T(8,128)S(1)} %shard_map.64) | data formatting | bytes 8192

commit v6 on v5

--- a/solution.py
+++ b/solution.py
@@ -17,8 +17,8 @@
 NT = (((1,), (1,)), ((), ()))
 NN = (((1,), (0,)), ((), ()))
 MESH = pl.DeviceIdType.MESH
-GROUPS = ((0, 112), (112, 96), (208, 48))
-GROUP_ENDS = (7, 13, 16)
+GROUPS = ((0, 80), (80, 96), (176, 80))
+GROUP_ENDS = (5, 11, 16)
 AWAY = (0, 1, 15, 2, 14, 3, 13, 4, 12, 5, 11, 6, 10, 7, 9, 8)
 Z_FAR = AWAY[:0:-1]
 OBS_FAR = (5, 4, 3, 7, 2, 6, 1, 0)

time: 46.1 us -> 45 us (0.976)
  Pallas kernels: 44.6 us -> 43.3 us
    pallas_call x1, Pallas kernels: 44.6 us -> 43.3 us  [body(): pl.pallas_call(kernel, out_shape=jax.ShapeDtypeStruct((8, 128), F32), in_...]
where the time goes in v6:
time: 45 us; the launch traced here: 44.6 us
  Pallas kernels  43.3 us (96%)
  between operations  0.66 us (1%)
  local copies, waits for them, and re-layouts  0.6 us (1%)
    pallas_call x1, Pallas kernels, body(): pl.pallas_call(kernel, out_shape=jax.ShapeDtypeStruct((8, 128), F32), in_...  43.3 us

profile of v6, /device:TPU:1, one launch (start us, length us, event | category | flops | bytes accessed | tf_op | source)
XLA Modules:
  0.0 44.6 jit_solution(17451174413621107203)
XLA Ops:
  0.7 43.3 %shard_map.64 = f32[8,128]{1,0:T(8,128)S(1)} custom-call(bf16[4000,128]{1,0:T(8,128)(2,1)} %bitcast.4, s32[1,1024]{1,0:T(1,128)} %bitcast.7, f32[3,1024]{1,0:T(4,128)} %coord_hbm.1, s32[64,128]{1,0:T(8,128)} %bitcast.6, bf16[2048,128]{1,0:T(8,128)(2,1)} %bitcast.5, s32[1,1]{1,0:T(1,128)S(6)} %copy.8.off_ref), custom_call_target="tpu_custom_call" | custom-call | tf_op jit(solution)/shard_map/pallas_call | solution.py:399
  44.0 0.6 %copy.9 = f32[8,128]{1,0:T(8,128)} copy(f32[8,128]{1,0:T(8,128)S(1)} %shard_map.64) | data formatting | bytes 8192

commit v7 on v6

--- a/solution.py
+++ b/solution.py
@@ -320,16 +320,20 @@
     def pieces(g, n):
         return held.at[0:n, pl.ds(*GROUPS[g])]
 
+    def pass_on(g):
+        settle(pieces(g, 3), Y_R + g)
+        for j in (2, 6, 4):
+            o_copy(g, bs[j], 1, O_R + g).start()
+
     for g in range(3):
+        if g == 2:
+            pass_on(0)
         first, size = GROUPS[g]
         skip = 16 if g == 0 else 0
         settle(held.at[b, pl.ds(first + skip, size - skip)], Z_R + g)
         for j in ((4, 2, 6, 1) if g < 2 else (5, 4, 3, 7, 2, 6, 1)):
             o_copy(g, b, j, Y_R + g if g < 2 and j > 1 else O_R + g).start()
-    for g in range(2):
-        settle(pieces(g, 3), Y_R + g)
-        for j in (2, 6, 4):
-            o_copy(g, bs[j], 1, O_R + g).start()
+    pass_on(1)
     for g in range(3):
         settle(pieces(g, 4 if g < 2 else 7), O_R + g)
 

time: 45 us -> 46.2 us (1.027)
  Pallas kernels: 43.3 us -> 44.5 us
    pallas_call x1, Pallas kernels: 43.3 us -> 44.5 us  [body(): pl.pallas_call(kernel, out_shape=jax.ShapeDtypeStruct((8, 128), F32), in_...]
where the time goes in v7:
time: 46.2 us; the launch traced here: 45.8 us
  Pallas kernels  44.5 us (96%)
  between operations  0.66 us (1%)
  local copies, waits for them, and re-layouts  0.6 us (1%)
    pallas_call x1, Pallas kernels, body(): pl.pallas_call(kernel, out_shape=jax.ShapeDtypeStruct((8, 128), F32), in_...  44.5 us

profile of v7, /device:TPU:1, one launch (start us, length us, event | category | flops | bytes accessed | tf_op | source)
XLA Modules:
  0.0 45.8 jit_solution(13077914624233867639)
XLA Ops:
  0.7 44.5 %shard_map.64 = f32[8,128]{1,0:T(8,128)S(1)} custom-call(bf16[4000,128]{1,0:T(8,128)(2,1)} %bitcast.4, s32[1,1024]{1,0:T(1,128)} %bitcast.7, f32[3,1024]{1,0:T(4,128)} %coord_hbm.1, s32[64,128]{1,0:T(8,128)} %bitcast.6, bf16[2048,128]{1,0:T(8,128)(2,1)} %bitcast.5, s32[1,1]{1,0:T(1,128)S(6)} %copy.8.off_ref), custom_call_target="tpu_custom_call" | custom-call | tf_op jit(solution)/shard_map/pallas_call | solution.py:403
  45.2 0.6 %copy.9 = f32[8,128]{1,0:T(8,128)} copy(f32[8,128]{1,0:T(8,128)S(1)} %shard_map.64) | data formatting | bytes 8192
